TPU v7x, 32 devices: a whole 2x2x4 slice. The times are simulated.
32 devices in a mesh: clique: 4 (over y, x), group: 8 (over z, core).
Axes of the slice: x: 2, y: 2, z: 4, core: 2. Of those that a mesh axis runs over, the one named last changes fastest.
Arguments:
- hot_shard: bfloat16 [65536, 128], P('clique'), may hold values from -6 to 6
- cold_shard: bfloat16 [131072, 128], P('group'), may hold values from -6 to 6
- hot_ids: int32 [32, 4, 512], P(('clique', 'group')), may hold values from 0 to 16383
- cold_ids: int32 [32, 8, 256], P(('clique', 'group')), may hold values from 0 to 16383
- cold_counts: int32 [32, 8], P(('clique', 'group')), may hold values from 128 to 256, as said below
- mid_self: int32 [32, 7680], P(('clique', 'group')), may hold values from 0 to 4095, as said below
- nbr1: int32 [32, 10, 7680], P(('clique', 'group')), may hold values from 0 to 4095, as said below
- nbr2: int32 [32, 15, 512], P(('clique', 'group')), may hold values from 0 to 7679
- labels: int32 [32, 512], P(('clique', 'group')), may hold values from 0 to 171
- w1_self: bfloat16 [128, 256], replicated, may hold values from -0.5 to 0.5
- w1_neigh: bfloat16 [128, 256], replicated, may hold values from -0.5 to 0.5
- w2_self: bfloat16 [256, 172], replicated, may hold values from -1.5 to 1.5
- w2_neigh: bfloat16 [256, 172], replicated, may hold values from -1.5 to 1.5
Outputs:
- seed_loss: float32 [32, 512], P(('clique', 'group'))
- grad_w1_self: float32 [128, 256], replicated
- grad_w1_neigh: float32 [128, 256], replicated
- grad_w2_self: float32 [256, 172], replicated
- grad_w2_neigh: float32 [256, 172], replicated
Inputs may be any that keep to these rules, and one draw needn't show every extreme that they name: `cold_counts`: the last store device has 256 live slots from every trainer; the other counts vary from store device to store device. `mid_self`: each entry is a position in the trainer's inputs that holds a hot row or a live cold slot. `nbr1`: each entry is a position in the trainer's inputs that holds a hot row or a live cold slot.
All inputs are finite; a program needn't handle non-finite values.
Results may differ from a plain program's by a relative error of at most 0.0021.
Values may be sent and summed in bfloat16 or wider, within the bound.
A program may use at most 128 MiB of HBM per device.

v0:
```python
from functools import partial

import jax
import jax.numpy as jnp
from jax import lax
from jax.sharding import PartitionSpec as P


def neighbour_total(positions, table):
    fan_count, middle = positions.shape
    table_rows = table.shape[0]
    row_block = 512
    columns = jnp.arange(table_rows, dtype=jnp.int32)[None, None, :]
    stacked = positions.reshape(fan_count, middle // row_block, row_block).transpose(1, 0, 2)

    def one_block(block_positions):
        matches = jnp.sum((block_positions[:, :, None] == columns).astype(jnp.float32), axis=0)
        return jnp.dot(matches.astype(jnp.bfloat16), table, preferred_element_type=jnp.float32)

    totals = lax.map(one_block, stacked)
    return totals.reshape(middle, table.shape[1])


def sage_step(
    self_first, neigh_first, seed_neigh, seed_labels, w1_self, w1_neigh, w2_self, w2_neigh
):
    seeds = seed_labels.shape[0]
    fan_second = seed_neigh.shape[0]
    middle = self_first.shape[0]
    classes = w2_self.shape[1]
    pre_first = jnp.dot(self_first, w1_self, preferred_element_type=jnp.float32) + jnp.dot(
        neigh_first, w1_neigh, preferred_element_type=jnp.float32
    )
    hidden_first = jax.nn.gelu(pre_first, approximate=True).astype(jnp.bfloat16)
    node_index = jnp.arange(middle, dtype=jnp.int32)[None, None, :]
    seed_counts = jnp.sum((seed_neigh[:, :, None] == node_index).astype(jnp.float32), axis=0)
    neigh_second = (
        jnp.dot(seed_counts.astype(jnp.bfloat16), hidden_first, preferred_element_type=jnp.float32)
        / fan_second
    ).astype(jnp.bfloat16)
    seed_hidden = hidden_first[:seeds]
    logits = jnp.dot(seed_hidden, w2_self, preferred_element_type=jnp.float32) + jnp.dot(
        neigh_second, w2_neigh, preferred_element_type=jnp.float32
    )
    log_total = jnp.log(jnp.sum(jnp.exp(logits), axis=1))
    picked = jnp.take_along_axis(logits, seed_labels[:, None], axis=1)[:, 0]
    seed_loss = log_total - picked
    onehot = (seed_labels[:, None] == jnp.arange(classes, dtype=jnp.int32)[None, :]).astype(
        jnp.float32
    )
    probs = jnp.exp(logits - log_total[:, None])
    grad_logits = ((probs - onehot) / seeds).astype(jnp.bfloat16)
    term_w2_self = jnp.dot(seed_hidden.T, grad_logits, preferred_element_type=jnp.float32)
    term_w2_neigh = jnp.dot(neigh_second.T, grad_logits, preferred_element_type=jnp.float32)
    back_second = jnp.dot(grad_logits, w2_neigh.T, preferred_element_type=jnp.float32) / fan_second
    grad_hidden = lax.dot_general(
        seed_counts,
        back_second,
        (((0,), (0,)), ((), ())),
        precision=lax.Precision.HIGHEST,
        preferred_element_type=jnp.float32,
    )
    grad_hidden = grad_hidden.at[:seeds].add(
        jnp.dot(grad_logits, w2_self.T, preferred_element_type=jnp.float32)
    )
    unused, pullback = jax.vjp(partial(jax.nn.gelu, approximate=True), pre_first)
    grad_pre = pullback(grad_hidden)[0].astype(jnp.bfloat16)
    term_w1_self = jnp.dot(self_first.T, grad_pre, preferred_element_type=jnp.float32)
    term_w1_neigh = jnp.dot(neigh_first.T, grad_pre, preferred_element_type=jnp.float32)
    return (seed_loss, term_w1_self, term_w1_neigh, term_w2_self, term_w2_neigh)


def body(
    hot_shard,
    cold_shard,
    hot_ids,
    cold_ids,
    cold_counts,
    mid_self,
    nbr1,
    nbr2,
    labels,
    w1_self,
    w1_neigh,
    w2_self,
    w2_neigh,
):
    feature_width = hot_shard.shape[1]
    requests = lax.all_to_all(hot_ids[0], "clique", split_axis=0, concat_axis=0, tiled=True)
    served = jnp.take(hot_shard, requests, axis=0)
    hot_rows = lax.all_to_all(served, "clique", split_axis=0, concat_axis=0, tiled=True).reshape(
        -1, feature_width
    )
    fetched = lax.all_to_all(
        jnp.take(
            cold_shard,
            lax.all_to_all(cold_ids[0], "group", split_axis=0, concat_axis=0, tiled=True),
            axis=0,
        ),
        "group",
        split_axis=0,
        concat_axis=0,
        tiled=True,
    )
    cold_slots = fetched.shape[1]
    live_mask = jnp.arange(cold_slots, dtype=jnp.int32)[None, :] < cold_counts[0][:, None]
    cold_rows = jnp.where(live_mask[:, :, None], fetched, jnp.zeros_like(fetched)).reshape(
        -1, feature_width
    )
    fan_first = nbr1.shape[1]
    inputs = jnp.concatenate([hot_rows, cold_rows], axis=0)
    self_first = jnp.take(inputs, mid_self[0], axis=0)
    summed = neighbour_total(nbr1[0], inputs)
    neigh_first = (summed / fan_first).astype(jnp.bfloat16)
    seed_loss, term_a, term_b, term_c, term_d = sage_step(
        self_first, neigh_first, nbr2[0], labels[0], w1_self, w1_neigh, w2_self, w2_neigh
    )
    totals = lax.psum((term_a, term_b, term_c, term_d), ("clique", "group"))
    return (seed_loss[None], totals[0], totals[1], totals[2], totals[3])


def solution(mesh):
    return jax.shard_map(
        body,
        mesh=mesh,
        in_specs=(
            P("clique", None),
            P("group", None),
            P(("clique", "group"), None, None),
            P(("clique", "group"), None, None),
            P(("clique", "group"), None),
            P(("clique", "group"), None),
            P(("clique", "group"), None, None),
            P(("clique", "group"), None, None),
            P(("clique", "group"), None),
            P(),
            P(),
            P(),
            P(),
        ),
        out_specs=(P(("clique", "group"), None), P(), P(), P(), P()),
        check_vma=False,
    )
```

profile of v0, /device:TPU:0, one launch (start us, length us, event | category | flops | bytes accessed | tf_op | source)
XLA Modules:
  0.0 817.0 jit_solution(13610457278303948443)
XLA Ops:
  8.5 6.3 all-to-all-start.2
  17.9 83.1 %convert_reduce_fusion.1 = f32[512,7680]{1,0:T(8,128)} fusion(s32[15,512]{1,0:T(8,128)S(1)} %bitcast.81), kind=kLoop, calls=%fused_computation.13 | loop fusion | flops 173015040 | bytes 15759360 | tf_op jit(solution)/shard_map/reduce_sum | solution.py:36
  105.4 8.3 %gather_fusion.1 = bf16[2048,128]{1,0:T(8,128)(2,1)S(1)} fusion(bf16[16384,128]{1,0:T(8,128)(2,1)} %param.18, s32[2048]{0:T(1024)S(1)} %broadcast_clamp_fusion), kind=kCustom, calls=%fused_computation.1 | custom fusion | bytes 1056768 | tf_op jit(solution)/shard_map/jit(_take)/gather | solution.py:95
  114.9 5.1 all-to-all-start.3
  120.1 8.3 %gather_fusion = bf16[2048,128]{1,0:T(8,128)(2,1)S(1)} fusion(bf16[16384,128]{1,0:T(8,128)(2,1)} %param.17, s32[2048]{0:T(1024)S(1)} %broadcast_clamp_fusion.1), kind=kCustom, calls=%fused_computation | custom fusion | bytes 1056768 | tf_op jit(solution)/shard_map/jit(_take)/gather | solution.py:90
  129.6 5.8 all-to-all-done.3
  135.4 4.2 all-to-all-start.1
  141.1 6.3 all-to-all-done.1
  147.5 14.4 %gather_fusion.2 = bf16[7680,128]{1,0:T(8,128)(2,1)S(1)} fusion(bf16[4096,128]{1,0:T(8,128)(2,1)S(1)} %pad_maximum_fusion, s32[8192]{0:T(1024)S(1)} %pad_clamp_fusion), kind=kCustom, calls=%fused_computation.2 | custom fusion | bytes 3962880 | tf_op jit(solution)/shard_map/jit(_take)/gather | solution.py:112
  161.9 451.1 %while.12 = (s32[]{:T(128)}, f32[15,512,128]{2,1,0:T(8,128)}, s32[15,10,512]{2,0,1:T(8,128)S(1)}, bf16[4096,128]{1,0:T(8,128)(2,1)S(1)}, s32[]{:T(128)}) while((s32[]{:T(128)}, f32[15,512,128]{2,1,0:T(8,128)}, s32[15,10,512]{2,0,1:T(8,128)S(1)}, bf16[4096,128]{1,0:T(8,128)(2,1)S(1)}, s32[]{:T(128)}) %tuple.41), condition=%wide.region_2.3_spmd.clone, body=%wide.region_0.0_spmd.clone.sunk | while | flops 597688320 | bytes 9801805 | solution.py:20
  161.9 25.9 %convert_reduce_fusion.3 = bf16[512,4096]{1,0:T(8,128)(2,1)} fusion(s32[10,512]{1,0:T(8,128)S(1)} %bitcast.75), kind=kLoop, calls=%fused_computation.6.clone.1 | loop fusion | flops 60817408 | bytes 4214784 | tf_op jit(solution)/shard_map/while/body/eval_jaxpr/reduce_sum | solution.py:17
  192.0 25.9 %convert_reduce_fusion.3 = bf16[512,4096]{1,0:T(8,128)(2,1)} fusion(s32[10,512]{1,0:T(8,128)S(1)} %bitcast.75), kind=kLoop, calls=%fused_computation.6.clone.1 | loop fusion | flops 60817408 | bytes 4214784 | tf_op jit(solution)/shard_map/while/body/eval_jaxpr/reduce_sum | solution.py:17
  222.1 25.9 %convert_reduce_fusion.3 = bf16[512,4096]{1,0:T(8,128)(2,1)} fusion(s32[10,512]{1,0:T(8,128)S(1)} %bitcast.75), kind=kLoop, calls=%fused_computation.6.clone.1 | loop fusion | flops 60817408 | bytes 4214784 | tf_op jit(solution)/shard_map/while/body/eval_jaxpr/reduce_sum | solution.py:17
  252.2 25.9 %convert_reduce_fusion.3 = bf16[512,4096]{1,0:T(8,128)(2,1)} fusion(s32[10,512]{1,0:T(8,128)S(1)} %bitcast.75), kind=kLoop, calls=%fused_computation.6.clone.1 | loop fusion | flops 60817408 | bytes 4214784 | tf_op jit(solution)/shard_map/while/body/eval_jaxpr/reduce_sum | solution.py:17
  282.2 25.9 %convert_reduce_fusion.3 = bf16[512,4096]{1,0:T(8,128)(2,1)} fusion(s32[10,512]{1,0:T(8,128)S(1)} %bitcast.75), kind=kLoop, calls=%fused_computation.6.clone.1 | loop fusion | flops 60817408 | bytes 4214784 | tf_op jit(solution)/shard_map/while/body/eval_jaxpr/reduce_sum | solution.py:17
  312.3 25.9 %convert_reduce_fusion.3 = bf16[512,4096]{1,0:T(8,128)(2,1)} fusion(s32[10,512]{1,0:T(8,128)S(1)} %bitcast.75), kind=kLoop, calls=%fused_computation.6.clone.1 | loop fusion | flops 60817408 | bytes 4214784 | tf_op jit(solution)/shard_map/while/body/eval_jaxpr/reduce_sum | solution.py:17
  342.4 25.9 %convert_reduce_fusion.3 = bf16[512,4096]{1,0:T(8,128)(2,1)} fusion(s32[10,512]{1,0:T(8,128)S(1)} %bitcast.75), kind=kLoop, calls=%fused_computation.6.clone.1 | loop fusion | flops 60817408 | bytes 4214784 | tf_op jit(solution)/shard_map/while/body/eval_jaxpr/reduce_sum | solution.py:17
  372.5 25.9 %convert_reduce_fusion.3 = bf16[512,4096]{1,0:T(8,128)(2,1)} fusion(s32[10,512]{1,0:T(8,128)S(1)} %bitcast.75), kind=kLoop, calls=%fused_computation.6.clone.1 | loop fusion | flops 60817408 | bytes 4214784 | tf_op jit(solution)/shard_map/while/body/eval_jaxpr/reduce_sum | solution.py:17
  402.5 25.9 %convert_reduce_fusion.3 = bf16[512,4096]{1,0:T(8,128)(2,1)} fusion(s32[10,512]{1,0:T(8,128)S(1)} %bitcast.75), kind=kLoop, calls=%fused_computation.6.clone.1 | loop fusion | flops 60817408 | bytes 4214784 | tf_op jit(solution)/shard_map/while/body/eval_jaxpr/reduce_sum | solution.py:17
  432.6 25.9 %convert_reduce_fusion.3 = bf16[512,4096]{1,0:T(8,128)(2,1)} fusion(s32[10,512]{1,0:T(8,128)S(1)} %bitcast.75), kind=kLoop, calls=%fused_computation.6.clone.1 | loop fusion | flops 60817408 | bytes 4214784 | tf_op jit(solution)/shard_map/while/body/eval_jaxpr/reduce_sum | solution.py:17
  462.7 25.9 %convert_reduce_fusion.3 = bf16[512,4096]{1,0:T(8,128)(2,1)} fusion(s32[10,512]{1,0:T(8,128)S(1)} %bitcast.75), kind=kLoop, calls=%fused_computation.6.clone.1 | loop fusion | flops 60817408 | bytes 4214784 | tf_op jit(solution)/shard_map/while/body/eval_jaxpr/reduce_sum | solution.py:17
  492.8 25.9 %convert_reduce_fusion.3 = bf16[512,4096]{1,0:T(8,128)(2,1)} fusion(s32[10,512]{1,0:T(8,128)S(1)} %bitcast.75), kind=kLoop, calls=%fused_computation.6.clone.1 | loop fusion | flops 60817408 | bytes 4214784 | tf_op jit(solution)/shard_map/while/body/eval_jaxpr/reduce_sum | solution.py:17
  522.8 25.9 %convert_reduce_fusion.3 = bf16[512,4096]{1,0:T(8,128)(2,1)} fusion(s32[10,512]{1,0:T(8,128)S(1)} %bitcast.75), kind=kLoop, calls=%fused_computation.6.clone.1 | loop fusion | flops 60817408 | bytes 4214784 | tf_op jit(solution)/shard_map/while/body/eval_jaxpr/reduce_sum | solution.py:17
  552.9 25.9 %convert_reduce_fusion.3 = bf16[512,4096]{1,0:T(8,128)(2,1)} fusion(s32[10,512]{1,0:T(8,128)S(1)} %bitcast.75), kind=kLoop, calls=%fused_computation.6.clone.1 | loop fusion | flops 60817408 | bytes 4214784 | tf_op jit(solution)/shard_map/while/body/eval_jaxpr/reduce_sum | solution.py:17
  583.0 25.9 %convert_reduce_fusion.3 = bf16[512,4096]{1,0:T(8,128)(2,1)} fusion(s32[10,512]{1,0:T(8,128)S(1)} %bitcast.75), kind=kLoop, calls=%fused_computation.6.clone.1 | loop fusion | flops 60817408 | bytes 4214784 | tf_op jit(solution)/shard_map/while/body/eval_jaxpr/reduce_sum | solution.py:17
  617.0 6.0 fusion.27
  623.0 6.6 multiply_convert_fusion
  630.9 4.4 fusion.23
  638.7 27.5 %fusion.39 = f32[7680,256]{1,0:T(8,128)S(1)} fusion(f32[512,7680]{1,0:T(8,128)S(1)} %bitcast.71, f32[512,256]{1,0:T(8,128)S(1)} %convolution_multiply_fusion), kind=kOutput, calls=%fused_computation.76 | convolution fusion | flops 12079595520 | bytes 24117248 | tf_op jit(solution)/shard_map/dot_general | solution.py:56
  666.6 5.3 fusion.16
  676.0 4.5 gather_fusion.3
  681.2 122.4 %all-reduce.3.cloned.1.call-done = (f32[128,256]{1,0:T(8,128)}, f32[128,256]{1,0:T(8,128)}, f32[256,172]{0,1:T(8,128)}, f32[256,172]{0,1:T(8,128)}) async-done(((f32[128,256]{1,0:T(8,128)}, f32[128,256]{1,0:T(8,128)}, f32[256,172]{0,1:T(8,128)}, f32[256,172]{0,1:T(8,128)}), (f32[128,256]{1,0:T(8,128)}, f32[128,256]{1,0:T(8,128)}, f32[256,172]{0,1:T(8,128)}, ...) | async-done | bytes 614416 | tf_op jit(solution)/shard_map/psum | solution.py:118
  (118 shorter events, 95.2 us)
Async XLA Ops:
  7.2 622.4 %copy-start = (bf16[256,172]{0,1:T(8,128)(2,1)S(1)}, bf16[256,172]{0,1:T(8,128)(2,1)}, u32[]{:S(2)}) copy-start(bf16[256,172]{0,1:T(8,128)(2,1)} %param.28) | copy-start | bytes 264196
  8.5 93.1 %all-to-all-start.2 = ((s32[8,1,256]{2,1,0:T(1,128)}), s32[8,1,256]{2,1,0:T(1,128)S(1)}, u32[]{:S(2)}, u32[]{:S(2)}) async-start(s32[8,1,256]{2,1,0:T(1,128)} %all_to_all.31), calls=%async_computation.2 | async-start | bytes 16384 | tf_op jit(solution)/shard_map/all_to_all | solution.py:97
  17.9 83.1 %copy-start.4 = (s32[1,7680]{1,0:T(1,128)S(1)}, s32[1,7680]{1,0:T(1,128)}, u32[]{:S(2)}) copy-start(s32[1,7680]{1,0:T(1,128)} %param.22) | copy-start | bytes 92164
  17.9 83.2 %copy-start.7 = (s32[1,4,512]{2,1,0:T(4,128)S(1)}, s32[1,4,512]{2,1,0:T(4,128)}, u32[]{:S(2)}) copy-start(s32[1,4,512]{2,1,0:T(4,128)} %param.19) | copy-start | bytes 24580
  100.9 38.9 %copy-start.3 = (s32[1,10,7680]{2,0,1:T(1,128)S(1)}, s32[1,10,7680]{2,0,1:T(1,128)}, u32[]{:S(2)}) copy-start(s32[1,10,7680]{2,0,1:T(1,128)} %param.23) | copy-start | bytes 921604
  101.7 13.3 %all-to-all-start = ((s32[4,1,512]{2,1,0:T(1,128)}), s32[4,1,512]{2,1,0:T(1,128)S(1)}, u32[]{:S(2)}, u32[]{:S(2)}) async-start(s32[4,1,512]{2,1,0:T(1,128)} %all_to_all.26), calls=%async_computation | async-start | bytes 16384 | tf_op jit(solution)/shard_map/all_to_all | solution.py:89
  114.9 20.5 %all-to-all-start.3 = ((bf16[8,256,128]{2,1,0:T(8,128)(2,1)}), bf16[8,256,128]{2,1,0:T(8,128)(2,1)S(1)}, u32[]{:S(2)}, u32[]{:S(2)}) async-start(bf16[8,256,128]{2,1,0:T(8,128)(2,1)} %broadcast_select_fusion.3), calls=%async_computation.3 | async-start | bytes 1048576 | tf_op jit(solution)/shard_map/all_to_all | solution.py:94
  135.4 12.0 %all-to-all-start.1 = ((bf16[4,512,128]{2,1,0:T(8,128)(2,1)}), bf16[4,512,128]{2,1,0:T(8,128)(2,1)S(1)}, u32[]{:S(2)}, u32[]{:S(2)}) async-start(bf16[4,512,128]{2,1,0:T(8,128)(2,1)} %broadcast_select_fusion.5), calls=%async_computation.1 | async-start | bytes 1048576 | tf_op jit(solution)/shard_map/all_to_all | solution.py:91
  139.6 664.0 %all-reduce.3.cloned.1.call-start = ((), (), s32[]{:S(2)}) async-start(), calls=%async_computation.4 | async-start | bytes 1245184 | tf_op jit(solution)/shard_map/psum | solution.py:118
  161.9 455.1 %copy-start.5 = (bf16[128,256]{1,0:T(8,128)(2,1)S(1)}, bf16[128,256]{1,0:T(8,128)(2,1)}, u32[]{:S(2)}) copy-start(bf16[128,256]{1,0:T(8,128)(2,1)} %param.26) | copy-start | bytes 196612
  616.9 6.0 copy-start.8
  616.9 13.9 %slice-start = ((s8[15728640]{0:T(1024)(128)(4,1)}), s8[4194304]{0:T(1024)(128)(4,1)S(1)}, s32[]{:S(2)}) async-start(s8[15728640]{0:T(1024)(128)(4,1)} %bitcast.70), calls=%async_computation.5 | async-start | bytes 8388608
  616.9 13.9 %slice-start.1 = ((s8[15728640]{0:T(1024)(128)(4,1)}), s8[4194304]{0:T(1024)(128)(4,1)S(1)}, s32[]{:S(2)}) async-start(s8[15728640]{0:T(1024)(128)(4,1)} %bitcast.70), calls=%async_computation.6 | async-start | bytes 8388608
  622.9 7.9 slice-start.2
  623.0 7.9 slice-start.3
  630.8 4.5 copy-start.2
  630.9 4.8 copy-start.6
  666.6 7.9 copy-start.1
Sparse Core Ops, SparseCore 0:
  676.1 127.4 all-reduce.2
where the time goes:
time: 823 us; the launch traced here: 817 us
  other arithmetic  487 us (59%)
  waiting for transfers between devices  135 us (16%)
  matrix products  116 us (14%)
  local copies, waits for them, and re-layouts  45.2 us (5%)
  starting transfers between devices  19.5 us (2%)
  between operations  14.6 us (2%)
    reduce_sum x15, other arithmetic, one_block(): jnp.sum((block_positions[:, :, None] == columns).astype(jnp.float32), axi...  388 us
    psum x1, waiting for transfers between devices, body(): totals = lax.psum((term_a, term_b, term_c, term_d), ('clique', 'group'))  122 us
    reduce_sum x1, other arithmetic, sage_step(): jnp.sum((seed_neigh[:, :, None] == node_index).astype(jnp.float32), axis=0)  83.1 us
    dot_general x15, matrix products, one_block(): jnp.dot(matches.astype(jnp.bfloat16), table, preferred_element_type=jnp.f...  62.3 us
    dot_general x1, matrix products, sage_step(): lax.dot_general(seed_counts, back_second, (((0,), (0,)), ((), ())), preci...  27.5 us
  transfers between devices with their start and end apart: 5, of which 3 were waited for; matrix products, arithmetic and copies ran while one was open for 14% of the time, Pallas kernels for 0%

commit v1 on v0

v1 whole, which is shorter than its diff:
```python
from functools import partial

import jax
import jax.numpy as jnp
from jax import lax
from jax.experimental import pallas as pl
from jax.experimental.pallas import tpu as pltpu
from jax.sharding import PartitionSpec as P

GELU_SCALE = 0.7978845608028654
GELU_CUBE = 0.044715
GRAD_ROWS = 1280
MESH = pl.DeviceIdType.MESH


def dot_first(left, right):
    return lax.dot_general(
        left, right, (((0,), (0,)), ((), ())), preferred_element_type=jnp.float32
    )


def dot_last(left, right):
    return lax.dot_general(
        left, right, (((1,), (1,)), ((), ())), preferred_element_type=jnp.float32
    )


def sage_kernel(
    counts_ref,
    self_ref,
    nbr1_ref,
    nbr2_ref,
    hot_ref,
    cold_ref,
    nbr2_vec_ref,
    labels_ref,
    w1_self_ref,
    w1_neigh_ref,
    w2_self_ref,
    w2_neigh_ref,
    loss_ref,
    grads_ref,
    table,
    spread_ids,
    self_rows,
    sum_rows,
    self_all,
    neigh_all,
    slope_all,
    hidden_all,
    counts_t,
    second_sum,
    w2_pad,
):
    step = pl.program_id(0)
    steps = pl.num_programs(0)
    fan_first, block = nbr1_ref.shape[1], nbr1_ref.shape[2]
    fan_second, seeds = nbr2_ref.shape[1], nbr2_ref.shape[2]
    owners, slots, width = cold_ref.shape
    hot_rows = hot_ref.shape[0]
    hidden = w1_self_ref.shape[1]
    classes = w2_self_ref.shape[1]
    padded = w2_pad.shape[2]

    @pl.when(step == 0)
    def _():
        table[0:hot_rows, :] = hot_ref[...].astype(jnp.float32)

        @pl.loop(0, owners)
        def _(owner):
            live = lax.broadcasted_iota(jnp.int32, (slots, width), 0) < counts_ref[0, owner]
            rows = cold_ref[owner].astype(jnp.float32)
            start = pl.multiple_of(hot_rows + owner * slots, 8)
            table[pl.ds(start, slots), :] = jnp.where(live, rows, 0.0)

        for k in range(fan_second):
            spread_ids[k] = jnp.broadcast_to(nbr2_vec_ref[0, k : k + 1, :], (8, seeds))
        w2_pad[...] = jnp.zeros_like(w2_pad)
        w2_pad[0, :, 0:classes] = w2_self_ref[...]
        w2_pad[1, :, 0:classes] = w2_neigh_ref[...]

    node_base = step * block

    @pl.loop(0, block // 16)
    def _(group):
        row = pl.multiple_of(group * 16, 16)
        for r in range(16):
            total = table[pl.ds(nbr1_ref[0, 0, row + r], 1), :]
            for k in range(1, fan_first):
                total = total + table[pl.ds(nbr1_ref[0, k, row + r], 1), :]
            sum_rows[pl.ds(row + r, 1), :] = total
            self_rows[pl.ds(row + r, 1), :] = table[pl.ds(self_ref[0, row + r], 1), :]
        halves = []
        for half in range(2):
            node = lax.broadcasted_iota(jnp.int32, (8, seeds), 0) + (node_base + row + half * 8)
            seen = jnp.zeros((8, seeds), jnp.float32)
            for k in range(fan_second):
                seen = seen + jnp.where(spread_ids[k] == node, 1.0, 0.0)
            halves.append(seen)
        counts_t[pl.ds(pl.multiple_of(node_base + row, 16), 16), :] = jnp.concatenate(
            halves, axis=0
        ).astype(jnp.bfloat16)

    here = pl.ds(pl.multiple_of(node_base, block), block)
    self_first = self_rows[...].astype(jnp.bfloat16)
    neigh_first = (sum_rows[...] / fan_first).astype(jnp.bfloat16)
    self_all[here, :] = self_first
    neigh_all[here, :] = neigh_first
    pre = jnp.dot(self_first, w1_self_ref[...], preferred_element_type=jnp.float32) + jnp.dot(
        neigh_first, w1_neigh_ref[...], preferred_element_type=jnp.float32
    )
    square = pre * pre
    bend = jnp.tanh(GELU_SCALE * (pre + GELU_CUBE * (square * pre)))
    half_up = 0.5 * (1.0 + bend)
    hidden_all[here, :] = (pre * half_up).astype(jnp.bfloat16).astype(jnp.float32)
    slope_all[here, :] = half_up + (0.5 * GELU_SCALE) * pre * (1.0 - bend * bend) * (
        1.0 + (3.0 * GELU_CUBE) * square
    )

    @pl.when(step == steps - 1)
    def _():
        @pl.loop(0, seeds // 8)
        def _(group):
            row = pl.multiple_of(group * 8, 8)
            for r in range(8):
                total = hidden_all[pl.ds(nbr2_ref[0, 0, row + r], 1), :]
                for k in range(1, fan_second):
                    total = total + hidden_all[pl.ds(nbr2_ref[0, k, row + r], 1), :]
                second_sum[pl.ds(row + r, 1), :] = total

        neigh_second = (second_sum[...] / fan_second).astype(jnp.bfloat16)
        seed_hidden = hidden_all[0:seeds, :].astype(jnp.bfloat16)
        w2_self = w2_pad[0]
        w2_neigh = w2_pad[1]
        logits = jnp.dot(seed_hidden, w2_self, preferred_element_type=jnp.float32) + jnp.dot(
            neigh_second, w2_neigh, preferred_element_type=jnp.float32
        )
        column = lax.broadcasted_iota(jnp.int32, (seeds, padded), 1)
        real = column < classes
        log_total = jnp.log(
            jnp.sum(jnp.where(real, jnp.exp(logits), 0.0), axis=1, keepdims=True)
        )
        label = jnp.transpose(jnp.broadcast_to(labels_ref[...], (128, seeds)))
        label = jnp.concatenate([label] * (padded // 128), axis=1)
        onehot = jnp.where(column == label, 1.0, 0.0)
        picked = jnp.sum(onehot * logits, axis=1, keepdims=True)
        loss = jnp.broadcast_to(log_total - picked, (seeds, 128))
        loss_ref[...] = jnp.transpose(loss)[0:1, :]
        probs = jnp.where(real, jnp.exp(logits - log_total), 0.0)
        grad_logits = ((probs - onehot) / seeds).astype(jnp.bfloat16)
        term_self = dot_first(seed_hidden, grad_logits)
        term_neigh = dot_first(neigh_second, grad_logits)
        at = 4 * width
        grads_ref[at : at + hidden, :] = term_self[:, 0:128]
        grads_ref[at + hidden : at + 2 * hidden, :] = term_neigh[:, 0:128]
        grads_ref[at + 2 * hidden : at + 3 * hidden, :] = term_self[:, 128:256] + pltpu.roll(
            term_neigh[:, 128:256], 64, 1
        )
        back_second = dot_last(grad_logits, w2_neigh) / fan_second
        back_high = back_second.astype(jnp.bfloat16)
        back_low = (back_second - back_high.astype(jnp.float32)).astype(jnp.bfloat16)
        second_sum[...] = dot_last(grad_logits, w2_self)

        grads_ref[0:at, :] = jnp.zeros((at, 128), jnp.float32)

        @pl.loop(0, steps)
        def _(part):
            rows = pl.ds(pl.multiple_of(part * block, block), block)
            seen = counts_t[rows, :]
            grad = jnp.dot(seen, back_high, preferred_element_type=jnp.float32) + jnp.dot(
                seen, back_low, preferred_element_type=jnp.float32
            )
            own = jnp.where(part == 0, 1.0, 0.0)
            grad = grad + own * second_sum[...]
            grad_pre = (grad * slope_all[rows, :]).astype(jnp.bfloat16)
            first = dot_first(self_all[rows, :], grad_pre)
            other = dot_first(neigh_all[rows, :], grad_pre)
            grads_ref[0:width, :] += first[:, 0:128]
            grads_ref[width : 2 * width, :] += first[:, 128:256]
            grads_ref[2 * width : 3 * width, :] += other[:, 0:128]
            grads_ref[3 * width : 4 * width, :] += other[:, 128:256]


def sage_step(hot_rows, cold_rows, counts, mid_self, nbr1, nbr2, labels, weights):
    w1_self, w1_neigh, w2_self, w2_neigh = weights
    seeds = labels.shape[1]
    middle = mid_self.shape[1]
    fan_first, fan_second = nbr1.shape[1], nbr2.shape[1]
    width, hidden = w1_self.shape
    block = seeds
    steps = middle // block
    table_rows = hot_rows.shape[0] + cold_rows.shape[0] * cold_rows.shape[1]
    vmem = pl.BlockSpec(memory_space=pltpu.VMEM)
    smem = pl.BlockSpec(memory_space=pltpu.SMEM)
    return pl.pallas_call(
        sage_kernel,
        grid=(steps,),
        out_shape=(
            jax.ShapeDtypeStruct((1, seeds), jnp.float32),
            jax.ShapeDtypeStruct((GRAD_ROWS, 128), jnp.float32),
        ),
        in_specs=[
            smem,
            pl.BlockSpec((1, block), lambda i: (0, i), memory_space=pltpu.SMEM),
            pl.BlockSpec((1, fan_first, block), lambda i: (0, 0, i), memory_space=pltpu.SMEM),
            smem,
        ]
        + [vmem] * 8,
        out_specs=(vmem, vmem),
        scratch_shapes=[
            pltpu.VMEM((table_rows, width), jnp.float32),
            pltpu.VMEM((fan_second, 8, seeds), jnp.int32),
            pltpu.VMEM((block, width), jnp.float32),
            pltpu.VMEM((block, width), jnp.float32),
            pltpu.VMEM((middle, width), jnp.bfloat16),
            pltpu.VMEM((middle, width), jnp.bfloat16),
            pltpu.VMEM((middle, hidden), jnp.float32),
            pltpu.VMEM((middle, hidden), jnp.float32),
            pltpu.VMEM((middle, seeds), jnp.bfloat16),
            pltpu.VMEM((seeds, hidden), jnp.float32),
            pltpu.VMEM((2, hidden, 256), jnp.bfloat16),
        ],
        compiler_params=pltpu.CompilerParams(vmem_limit_bytes=52 * 1024 * 1024),
        name="sage_step",
    )(
        counts, mid_self, nbr1, nbr2,
        hot_rows, cold_rows, nbr2, labels, w1_self, w1_neigh, w2_self, w2_neigh,
    )


def reduce_kernel(
    cliques,
    groups,
    term_ref,
    w1_self_ref,
    w1_neigh_ref,
    w2_self_ref,
    w2_neigh_ref,
    whole,
    pair_in,
    clique_in,
    chip_in,
    half_sum,
    back,
    pair_sems,
    clique_sems,
    chip_sems,
):
    chips = groups // 2
    c = lax.axis_index("clique")
    g = lax.axis_index("group")
    core = lax.rem(g, 2)
    chip = g // 2
    rows = whole.shape[0]
    per_pair = rows // 2
    per_clique = per_pair // cliques
    per_chip = per_clique // chips

    def pair():
        return (c, chip * 2 + 1 - core)

    def clique(d):
        return (lax.rem(c + d, cliques), g)

    def other_chip(d):
        return (c, lax.rem(chip + d, chips) * 2 + core)

    def rows_at(start, size):
        return pl.ds(pl.multiple_of(start, 8), size)

    def send(source, target, sems, number, device):
        copy = pltpu.make_async_remote_copy(
            src_ref=source,
            dst_ref=target,
            send_sem=sems.at[0, number],
            recv_sem=sems.at[1, number],
            device_id=device,
            device_id_type=MESH,
        )
        copy.start()
        return copy

    barrier = pltpu.get_barrier_semaphore()
    partners = [pair()]
    partners += [clique(d) for d in range(1, cliques)]
    partners += [other_chip(d) for d in range(1, chips)]
    for device in partners:
        pl.semaphore_signal(barrier, inc=1, device_id=device, device_id_type=MESH)
    terms = term_ref.shape[0]
    whole[0:terms, :] = term_ref[...]
    if rows > terms:
        whole[terms:rows, :] = jnp.zeros((rows - terms, 128), jnp.float32)
    pl.semaphore_wait(barrier, len(partners))

    pair_start = core * per_pair
    mine = pair_start + c * per_clique
    own = mine + chip * per_chip

    copy = send(
        whole.at[rows_at((1 - core) * per_pair, per_pair)], pair_in, pair_sems, 0, pair()
    )
    copy.wait()
    half = rows_at(pair_start, per_pair)
    half_sum[half, :] = whole[half, :] + pair_in[...]

    copies = []
    for d in range(1, cliques):
        peer = lax.rem(c + d, cliques)
        part = rows_at(pair_start + peer * per_clique, per_clique)
        copies.append(send(half_sum.at[part], clique_in.at[d - 1], clique_sems, d - 1, clique(d)))
    for copy in copies:
        copy.wait()
    part = rows_at(mine, per_clique)
    total = half_sum[part, :]
    for d in range(1, cliques):
        total = total + clique_in[d - 1]
    whole[part, :] = total

    copies = []
    for d in range(1, chips):
        peer = lax.rem(chip + d, chips)
        part = rows_at(mine + peer * per_chip, per_chip)
        copies.append(send(whole.at[part], chip_in.at[d - 1], chip_sems, d - 1, other_chip(d)))
    for copy in copies:
        copy.wait()
    part = rows_at(own, per_chip)
    total = whole[part, :]
    for d in range(1, chips):
        total = total + chip_in[d - 1]
    back[part, :] = total

    copies = []
    for d in range(1, chips):
        copies.append(
            send(back.at[part], back.at[part], chip_sems, chips - 2 + d, other_chip(d))
        )
    for copy in copies:
        copy.wait()
    part = rows_at(mine, per_clique)
    copies = []
    for d in range(1, cliques):
        copies.append(
            send(back.at[part], back.at[part], clique_sems, cliques - 2 + d, clique(d))
        )
    for copy in copies:
        copy.wait()
    part = rows_at(pair_start, per_pair)
    copy = send(back.at[part], back.at[part], pair_sems, 1, pair())
    copy.wait()

    width, hidden = w1_self_ref.shape
    tail = w2_self_ref.shape[1] - 128
    w1_self_ref[:, 0:128] = back[0:width, :]
    w1_self_ref[:, 128:256] = back[width : 2 * width, :]
    w1_neigh_ref[:, 0:128] = back[2 * width : 3 * width, :]
    w1_neigh_ref[:, 128:256] = back[3 * width : 4 * width, :]
    at = 4 * width
    w2_self_ref[:, 0:128] = back[at : at + hidden, :]
    w2_neigh_ref[:, 0:128] = back[at + hidden : at + 2 * hidden, :]
    tails = back[at + 2 * hidden : at + 3 * hidden, :]
    w2_self_ref[:, 128 : 128 + tail] = tails[:, 0:tail]
    w2_neigh_ref[:, 128 : 128 + tail] = pltpu.roll(tails, 64, 1)[:, 0:tail]


def reduce_terms(terms, shapes, cliques, groups):
    chips = groups // 2
    unit = 8 * 2 * cliques * chips
    rows = -(-terms.shape[0] // unit) * unit
    per_clique = rows // 2 // cliques
    vmem = pl.BlockSpec(memory_space=pltpu.VMEM)
    return pl.pallas_call(
        partial(reduce_kernel, cliques, groups),
        out_shape=tuple(jax.ShapeDtypeStruct(shape, jnp.float32) for shape in shapes),
        in_specs=[vmem],
        out_specs=(vmem,) * len(shapes),
        scratch_shapes=[
            pltpu.VMEM((rows, 128), jnp.float32),
            pltpu.VMEM((rows // 2, 128), jnp.float32),
            pltpu.VMEM((cliques - 1, per_clique, 128), jnp.float32),
            pltpu.VMEM((chips - 1, per_clique // chips, 128), jnp.float32),
            pltpu.VMEM((rows, 128), jnp.float32),
            pltpu.VMEM((rows, 128), jnp.float32),
            pltpu.SemaphoreType.DMA((2, 2)),
            pltpu.SemaphoreType.DMA((2, 2 * (cliques - 1))),
            pltpu.SemaphoreType.DMA((2, 2 * (chips - 1))),
        ],
        compiler_params=pltpu.CompilerParams(
            collective_id=0, has_side_effects=True, vmem_limit_bytes=32 * 1024 * 1024
        ),
        name="reduce_terms",
    )(terms)


def body(
    cliques,
    groups,
    hot_shard,
    cold_shard,
    hot_ids,
    cold_ids,
    cold_counts,
    mid_self,
    nbr1,
    nbr2,
    labels,
    w1_self,
    w1_neigh,
    w2_self,
    w2_neigh,
):
    width = hot_shard.shape[1]
    requests = lax.all_to_all(hot_ids[0], "clique", split_axis=0, concat_axis=0, tiled=True)
    served = jnp.take(hot_shard, requests, axis=0)
    hot_rows = lax.all_to_all(served, "clique", split_axis=0, concat_axis=0, tiled=True).reshape(
        -1, width
    )
    fetched = lax.all_to_all(
        jnp.take(
            cold_shard,
            lax.all_to_all(cold_ids[0], "group", split_axis=0, concat_axis=0, tiled=True),
            axis=0,
        ),
        "group",
        split_axis=0,
        concat_axis=0,
        tiled=True,
    )
    seed_loss, terms = sage_step(
        hot_rows, fetched, cold_counts, mid_self, nbr1, nbr2, labels,
        (w1_self, w1_neigh, w2_self, w2_neigh),
    )
    shapes = (w1_self.shape, w1_neigh.shape, w2_self.shape, w2_neigh.shape)
    totals = reduce_terms(terms, shapes, cliques, groups)
    return (seed_loss, totals[0], totals[1], totals[2], totals[3])


def solution(mesh):
    return jax.shard_map(
        partial(body, mesh.shape["clique"], mesh.shape["group"]),
        mesh=mesh,
        in_specs=(
            P("clique", None),
            P("group", None),
            P(("clique", "group"), None, None),
            P(("clique", "group"), None, None),
            P(("clique", "group"), None),
            P(("clique", "group"), None),
            P(("clique", "group"), None, None),
            P(("clique", "group"), None, None),
            P(("clique", "group"), None),
            P(),
            P(),
            P(),
            P(),
        ),
        out_specs=(P(("clique", "group"), None), P(), P(), P(), P()),
        check_vma=False,
    )
```

time: 823 us -> 244 us (0.30)
  other arithmetic: 487 us -> 2.33 us
  Pallas kernels: 0 us -> 179 us
  waiting for transfers between devices: 135 us -> 18.4 us
  matrix products: 116 us -> 0 us
  local copies, waits for them, and re-layouts: 45.2 us -> 23.5 us
  between operations: 14.6 us -> 0.84 us
    reduce_sum x16 -> x0, other arithmetic: 471 us -> none  [the longest x15 388 us: one_block(): jnp.sum((block_positions[:, :, None] == columns).astype(jnp.float32), axi...]
    pallas_call x0 -> x2, Pallas kernels: none -> 179 us  [the longest x1 155 us: sage_step(): pl.pallas_call(sage_kernel, grid=(steps,), out_shape=(jax.ShapeDtypeStruc...]
    psum x1 -> x0, waiting for transfers between devices: 122 us -> none  [body(): totals = lax.psum((term_a, term_b, term_c, term_d), ('clique', 'group'))]
    dot_general x27 -> x0, matrix products: 116 us -> none  [the longest x15 62.3 us: one_block(): jnp.dot(matches.astype(jnp.bfloat16), table, preferred_element_type=jnp.f...]
    gather x2 -> x0, local copies, waits for them, and re-layouts: 18.9 us -> none  [the longest x1 14.4 us: body(): self_first = jnp.take(inputs, mid_self[0], axis=0)]
    convert_element_type x3 -> x0, other arithmetic: 9.35 us -> none  [the longest x1 5.31 us: sage_step(): grad_pre = pullback(grad_hidden)[0].astype(jnp.bfloat16)]
    all_to_all x1, waiting for transfers between devices: 5.84 us -> 15 us  [body(): lax.all_to_all(jnp.take(cold_shard, lax.all_to_all(cold_ids[0], 'group',...]
  transfers between devices with their start and end apart: 5 -> 4, of which waited for: 3 -> 2; matrix products, arithmetic and copies ran while one was open for 14% -> 8% of each run, Pallas kernels for 0% -> 0%
where the time goes in v1:
time: 244 us; the launch traced here: 243 us
  Pallas kernels  179 us (73%)
  local copies, waits for them, and re-layouts  23.5 us (10%)
  starting transfers between devices  18.8 us (8%)
  waiting for transfers between devices  18.4 us (8%)
    pallas_call x1, Pallas kernels, sage_step(): pl.pallas_call(sage_kernel, grid=(steps,), out_shape=(jax.ShapeDtypeStruc...  155 us
    pallas_call x1, Pallas kernels, reduce_terms(): pl.pallas_call(partial(reduce_kernel, cliques, groups), out_shape=tuple((...  23.7 us
    all_to_all x1, waiting for transfers between devices, body(): lax.all_to_all(jnp.take(cold_shard, lax.all_to_all(cold_ids[0], 'group',...  15 us
    gather x1, local copies, waits for them, and re-layouts, body(): jnp.take(cold_shard, lax.all_to_all(cold_ids[0], 'group', split_axis=0, c...  8.35 us
    gather x1, local copies, waits for them, and re-layouts, body(): served = jnp.take(hot_shard, requests, axis=0)  8.33 us
    all_to_all x1, starting transfers between devices, body(): lax.all_to_all(hot_ids[0], 'clique', split_axis=0, concat_axis=0, tiled=T...  5.16 us
    all_to_all x1, starting transfers between devices, body(): lax.all_to_all(jnp.take(cold_shard, lax.all_to_all(cold_ids[0], 'group',...  5.1 us
  transfers between devices with their start and end apart: 4, of which 2 were waited for; matrix products, arithmetic and copies ran while one was open for 8% of the time, Pallas kernels for 0%

profile of v1, /device:TPU:0, one launch (start us, length us, event | category | flops | bytes accessed | tf_op | source)
XLA Modules:
  0.0 242.9 jit_solution(11246033726624624324)
XLA Ops:
  0.6 1.3 all_to_all.26
  1.9 5.2 %all-to-all-start = ((s32[4,1,512]{2,1,0:T(1,128)}), s32[4,1,512]{2,1,0:T(1,128)S(1)}, u32[]{:S(2)}, u32[]{:S(2)}) async-start(s32[4,1,512]{2,1,0:T(1,128)} %all_to_all.26), calls=%async_computation | async-start | bytes 16384 | tf_op jit(solution)/shard_map/all_to_all | solution.py:412
  7.1 1.3 all_to_all.31
  8.4 3.4 %all-to-all-done = s32[4,1,512]{2,1,0:T(1,128)S(1)} async-done(((s32[4,1,512]{2,1,0:T(1,128)}), s32[4,1,512]{2,1,0:T(1,128)S(1)}, u32[]{:S(2)}, u32[]{:S(2)}) %all-to-all-start) | async-done | bytes 8224 | tf_op jit(solution)/shard_map/all_to_all | solution.py:412
  11.8 4.9 %all-to-all-start.2 = ((s32[8,1,256]{2,1,0:T(1,128)}), s32[8,1,256]{2,1,0:T(1,128)S(1)}, u32[]{:S(2)}, u32[]{:S(2)}) async-start(s32[8,1,256]{2,1,0:T(1,128)} %all_to_all.31), calls=%async_computation.2 | async-start | bytes 16384 | tf_op jit(solution)/shard_map/all_to_all | solution.py:420
  16.7 8.3 %gather_fusion = bf16[2048,128]{1,0:T(8,128)(2,1)S(1)} fusion(bf16[16384,128]{1,0:T(8,128)(2,1)} %param.13, s32[2048]{0:T(1024)S(1)} %broadcast_clamp_fusion.1), kind=kCustom, calls=%fused_computation | custom fusion | bytes 1056768 | tf_op jit(solution)/shard_map/jit(_take)/gather | solution.py:413
  25.0 1.1 broadcast_select_fusion.1
  26.2 0.0 all-to-all-done.2
  26.2 3.6 %all-to-all-start.1 = ((bf16[4,512,128]{2,1,0:T(8,128)(2,1)}), bf16[4,512,128]{2,1,0:T(8,128)(2,1)S(1)}, u32[]{:S(2)}, u32[]{:S(2)}) async-start(bf16[4,512,128]{2,1,0:T(8,128)(2,1)} %broadcast_select_fusion.1), calls=%async_computation.1 | async-start | bytes 1048576 | tf_op jit(solution)/shard_map/all_to_all | solution.py:414
  29.8 0.0 copy-start.1
  29.8 0.0 copy-start.2
  29.9 0.0 copy-start.3
  29.9 0.0 copy-start.4
  29.9 0.0 copy-start.5
  29.9 8.3 %gather_fusion.1 = bf16[2048,128]{1,0:T(8,128)(2,1)S(1)} fusion(bf16[16384,128]{1,0:T(8,128)(2,1)} %param.14, s32[2048]{0:T(1024)S(1)} %broadcast_clamp_fusion), kind=kCustom, calls=%fused_computation.1 | custom fusion | bytes 1056768 | tf_op jit(solution)/shard_map/jit(_take)/gather | solution.py:418
  38.3 1.1 broadcast_select_fusion
  39.4 0.0 all-to-all-done.1
  39.4 5.1 %all-to-all-start.3 = ((bf16[8,256,128]{2,1,0:T(8,128)(2,1)}), bf16[8,256,128]{2,1,0:T(8,128)(2,1)S(1)}, u32[]{:S(2)}, u32[]{:S(2)}) async-start(bf16[8,256,128]{2,1,0:T(8,128)(2,1)} %broadcast_select_fusion), calls=%async_computation.3 | async-start | bytes 1048576 | tf_op jit(solution)/shard_map/all_to_all | solution.py:417
  44.5 0.0 copy-done.9
  44.6 0.0 copy-done.7
  44.6 0.1 copy.28.w2_self_ref
  44.7 0.0 copy-done.8
  44.7 0.1 copy.29.w2_neigh_ref
  44.8 15.0 %all-to-all-done.3.cold_ref = bf16[8,256,128]{2,1,0:T(8,128)(2,1)S(1)} async-done(((bf16[8,256,128]{2,1,0:T(8,128)(2,1)}), bf16[8,256,128]{2,1,0:T(8,128)(2,1)S(1)}, u32[]{:S(2)}, u32[]{:S(2)}) %all-to-all-start.3) | async-done | bytes 524320 | tf_op jit(solution)/shard_map/all_to_all | solution.py:417
  59.9 0.0 copy-done.2
  59.9 155.3 %sage_step.1 = (f32[1,512]{1,0:T(1,128)}, f32[1280,128]{1,0:T(8,128)}) custom-call(s32[1,8]{1,0:T(1,128)S(1)} %copy-done.5, s32[1,7680]{1,0:T(1,128)S(1)} %copy-done.3, s32[1,10,7680]{2,1,0:T(8,128)S(1)} %copy.25.nbr1_ref, s32[1,15,512]{2,1,0:T(8,128)S(1)} %copy.26.nbr2_ref.nbr2_vec_ref, bf16[2048,128]{1,0:T(8,128)(2,1)S(1)} %bitcast.17, ...), custom_call_target="tpu_custom_call" | custom-call | tf_op jit(solution)/shard_map/sage_step/pallas_call | solution.py:195
  215.3 1.1 copy-done
  216.3 23.7 %reduce_terms.1 = (f32[128,256]{1,0:T(8,128)S(1)}, f32[128,256]{1,0:T(8,128)S(1)}, f32[256,172]{1,0:T(8,128)S(1)}, f32[256,172]{1,0:T(8,128)S(1)}) custom-call(f32[1280,128]{1,0:T(8,128)S(1)} %copy-done), custom_call_target="tpu_custom_call" | custom-call | tf_op jit(solution)/shard_map/reduce_terms/pallas_call | solution.py:371
  240.1 0.8 copy.30
  240.8 0.8 copy.31
  241.6 0.7 copy.42
  242.3 0.7 copy.43
  (18 shorter events, 0.1 us)
Async XLA Ops:
  1.9 9.9 %all-to-all-start = ((s32[4,1,512]{2,1,0:T(1,128)}), s32[4,1,512]{2,1,0:T(1,128)S(1)}, u32[]{:S(2)}, u32[]{:S(2)}) async-start(s32[4,1,512]{2,1,0:T(1,128)} %all_to_all.26), calls=%async_computation | async-start | bytes 16384 | tf_op jit(solution)/shard_map/all_to_all | solution.py:412
  11.8 14.4 %all-to-all-start.2 = ((s32[8,1,256]{2,1,0:T(1,128)}), s32[8,1,256]{2,1,0:T(1,128)S(1)}, u32[]{:S(2)}, u32[]{:S(2)}) async-start(s32[8,1,256]{2,1,0:T(1,128)} %all_to_all.31), calls=%async_computation.2 | async-start | bytes 16384 | tf_op jit(solution)/shard_map/all_to_all | solution.py:420
  26.2 18.3 %copy-start.9 = (s32[1,15,512]{2,0,1:T(1,128)S(1)}, s32[1,15,512]{2,0,1:T(1,128)}, u32[]{:S(2)}) copy-start(s32[1,15,512]{2,0,1:T(1,128)} %param.20) | copy-start | bytes 92164
  26.2 18.4 %copy-start.7 = (bf16[256,172]{0,1:T(8,128)(2,1)S(1)}, bf16[256,172]{0,1:T(8,128)(2,1)}, u32[]{:S(2)}) copy-start(bf16[256,172]{0,1:T(8,128)(2,1)} %param.24) | copy-start | bytes 264196
  26.2 18.5 %copy-start.8 = (bf16[256,172]{0,1:T(8,128)(2,1)S(1)}, bf16[256,172]{0,1:T(8,128)(2,1)}, u32[]{:S(2)}) copy-start(bf16[256,172]{0,1:T(8,128)(2,1)} %param.25) | copy-start | bytes 264196
  26.2 18.6 %copy-start.6 = (s32[1,10,7680]{2,0,1:T(1,128)S(1)}, s32[1,10,7680]{2,0,1:T(1,128)}, u32[]{:S(2)}) copy-start(s32[1,10,7680]{2,0,1:T(1,128)} %param.19) | copy-start | bytes 921604
  26.2 13.2 %all-to-all-start.1 = ((bf16[4,512,128]{2,1,0:T(8,128)(2,1)}), bf16[4,512,128]{2,1,0:T(8,128)(2,1)S(1)}, u32[]{:S(2)}, u32[]{:S(2)}) async-start(bf16[4,512,128]{2,1,0:T(8,128)(2,1)} %broadcast_select_fusion.1), calls=%async_computation.1 | async-start | bytes 1048576 | tf_op jit(solution)/shard_map/all_to_all | solution.py:414
  29.8 30.1 %copy-start.1 = (bf16[128,256]{1,0:T(8,128)(2,1)S(1)}, bf16[128,256]{1,0:T(8,128)(2,1)}, u32[]{:S(2)}) copy-start(bf16[128,256]{1,0:T(8,128)(2,1)} %w1_self_ref.1) | copy-start | bytes 196612
  29.8 30.1 %copy-start.2 = (bf16[128,256]{1,0:T(8,128)(2,1)S(1)}, bf16[128,256]{1,0:T(8,128)(2,1)}, u32[]{:S(2)}) copy-start(bf16[128,256]{1,0:T(8,128)(2,1)} %w1_neigh_ref.1) | copy-start | bytes 196612
  29.9 30.0 %copy-start.3 = (s32[1,7680]{1,0:T(1,128)S(1)}, s32[1,7680]{1,0:T(1,128)}, u32[]{:S(2)}) copy-start(s32[1,7680]{1,0:T(1,128)} %self_ref.1) | copy-start | bytes 92164
  29.9 30.0 %copy-start.4 = (s32[1,512]{1,0:T(1,128)S(1)}, s32[1,512]{1,0:T(1,128)}, u32[]{:S(2)}) copy-start(s32[1,512]{1,0:T(1,128)} %labels_ref.1) | copy-start | bytes 6148
  29.9 30.0 %copy-start.5 = (s32[1,8]{1,0:T(1,128)S(1)}, s32[1,8]{1,0:T(1,128)}, u32[]{:S(2)}) copy-start(s32[1,8]{1,0:T(1,128)} %counts_ref.1) | copy-start | bytes 100
  39.4 20.5 %all-to-all-start.3 = ((bf16[8,256,128]{2,1,0:T(8,128)(2,1)}), bf16[8,256,128]{2,1,0:T(8,128)(2,1)S(1)}, u32[]{:S(2)}, u32[]{:S(2)}) async-start(bf16[8,256,128]{2,1,0:T(8,128)(2,1)} %broadcast_select_fusion), calls=%async_computation.3 | async-start | bytes 1048576 | tf_op jit(solution)/shard_map/all_to_all | solution.py:417
  215.3 1.1 copy-start

commit v2 on v1

--- a/solution.py
+++ b/solution.py
@@ -29,10 +29,9 @@
     counts_ref,
     self_ref,
     nbr1_ref,
-    nbr2_ref,
     hot_ref,
     cold_ref,
-    nbr2_vec_ref,
+    nbr2_ref,
     labels_ref,
     w1_self_ref,
     w1_neigh_ref,
@@ -44,19 +43,23 @@
     spread_ids,
     self_rows,
     sum_rows,
-    self_all,
-    neigh_all,
+    first_all,
     slope_all,
-    hidden_all,
     counts_t,
-    second_sum,
+    seed_hidden_ref,
+    second_t,
+    seed_grad,
+    w1_both,
     w2_pad,
+    grad_w1,
 ):
     step = pl.program_id(0)
     steps = pl.num_programs(0)
-    fan_first, block = nbr1_ref.shape[1], nbr1_ref.shape[2]
+    groups, unit, width = sum_rows.shape
+    block = groups * unit
+    fan_first = nbr1_ref.shape[0] // block
     fan_second, seeds = nbr2_ref.shape[1], nbr2_ref.shape[2]
-    owners, slots, width = cold_ref.shape
+    owners, slots, _ = cold_ref.shape
     hot_rows = hot_ref.shape[0]
     hidden = w1_self_ref.shape[1]
     classes = w2_self_ref.shape[1]
@@ -64,72 +67,72 @@
 
     @pl.when(step == 0)
     def _():
-        table[0:hot_rows, :] = hot_ref[...].astype(jnp.float32)
+        @pl.loop(0, hot_rows // 16)
+        def _(part):
+            rows = hot_ref[pl.ds(pl.multiple_of(part * 16, 16), 16), :].astype(jnp.float32)
+            for r in range(16):
+                table[part * 16 + r] = rows[r : r + 1, :]
 
         @pl.loop(0, owners)
         def _(owner):
             live = lax.broadcasted_iota(jnp.int32, (slots, width), 0) < counts_ref[0, owner]
-            rows = cold_ref[owner].astype(jnp.float32)
-            start = pl.multiple_of(hot_rows + owner * slots, 8)
-            table[pl.ds(start, slots), :] = jnp.where(live, rows, 0.0)
+            rows = jnp.where(live, cold_ref[owner].astype(jnp.float32), 0.0)
+            for r in range(slots):
+                table[hot_rows + owner * slots + r] = rows[r : r + 1, :]
 
         for k in range(fan_second):
-            spread_ids[k] = jnp.broadcast_to(nbr2_vec_ref[0, k : k + 1, :], (8, seeds))
+            spread_ids[k] = jnp.broadcast_to(nbr2_ref[0, k : k + 1, :], (8, seeds))
+        w1_both[0:width, :] = w1_self_ref[...]
+        w1_both[width : 2 * width, :] = w1_neigh_ref[...]
         w2_pad[...] = jnp.zeros_like(w2_pad)
         w2_pad[0, :, 0:classes] = w2_self_ref[...]
         w2_pad[1, :, 0:classes] = w2_neigh_ref[...]
+        second_t[...] = jnp.zeros_like(second_t)
 
     node_base = step * block
 
-    @pl.loop(0, block // 16)
+    @pl.loop(0, groups)
     def _(group):
-        row = pl.multiple_of(group * 16, 16)
-        for r in range(16):
-            total = table[pl.ds(nbr1_ref[0, 0, row + r], 1), :]
+        row = group * unit
+        for r in range(unit):
+            total = table[nbr1_ref[row + r]]
             for k in range(1, fan_first):
-                total = total + table[pl.ds(nbr1_ref[0, k, row + r], 1), :]
-            sum_rows[pl.ds(row + r, 1), :] = total
-            self_rows[pl.ds(row + r, 1), :] = table[pl.ds(self_ref[0, row + r], 1), :]
+                total = total + table[nbr1_ref[row + (k * block + r)]]
+            sum_rows[group, r : r + 1, :] = total
+            self_rows[group, r : r + 1, :] = table[self_ref[node_base + row + r]]
         halves = []
-        for half in range(2):
+        for half in range(unit // 8):
             node = lax.broadcasted_iota(jnp.int32, (8, seeds), 0) + (node_base + row + half * 8)
             seen = jnp.zeros((8, seeds), jnp.float32)
             for k in range(fan_second):
                 seen = seen + jnp.where(spread_ids[k] == node, 1.0, 0.0)
             halves.append(seen)
-        counts_t[pl.ds(pl.multiple_of(node_base + row, 16), 16), :] = jnp.concatenate(
-            halves, axis=0
-        ).astype(jnp.bfloat16)
+        counts_t[step * groups + group] = jnp.concatenate(halves, axis=0).astype(jnp.bfloat16)
 
     here = pl.ds(pl.multiple_of(node_base, block), block)
-    self_first = self_rows[...].astype(jnp.bfloat16)
-    neigh_first = (sum_rows[...] / fan_first).astype(jnp.bfloat16)
-    self_all[here, :] = self_first
-    neigh_all[here, :] = neigh_first
-    pre = jnp.dot(self_first, w1_self_ref[...], preferred_element_type=jnp.float32) + jnp.dot(
-        neigh_first, w1_neigh_ref[...], preferred_element_type=jnp.float32
-    )
+    self_first = self_rows[...].reshape(block, width).astype(jnp.bfloat16)
+    neigh_first = (sum_rows[...].reshape(block, width) / fan_first).astype(jnp.bfloat16)
+    first = jnp.concatenate([self_first, neigh_first], axis=1)
+    first_all[here, :] = first
+    pre = jnp.dot(first, w1_both[...], preferred_element_type=jnp.float32)
     square = pre * pre
     bend = jnp.tanh(GELU_SCALE * (pre + GELU_CUBE * (square * pre)))
     half_up = 0.5 * (1.0 + bend)
-    hidden_all[here, :] = (pre * half_up).astype(jnp.bfloat16).astype(jnp.float32)
+    hidden_first = (pre * half_up).astype(jnp.bfloat16)
     slope_all[here, :] = half_up + (0.5 * GELU_SCALE) * pre * (1.0 - bend * bend) * (
         1.0 + (3.0 * GELU_CUBE) * square
     )
+    seen = counts_t[pl.ds(step * groups, groups)].reshape(block, seeds)
+    second_t[...] += dot_first(hidden_first, seen)
+
+    @pl.when(step == 0)
+    def _():
+        seed_hidden_ref[...] = hidden_first
 
     @pl.when(step == steps - 1)
     def _():
-        @pl.loop(0, seeds // 8)
-        def _(group):
-            row = pl.multiple_of(group * 8, 8)
-            for r in range(8):
-                total = hidden_all[pl.ds(nbr2_ref[0, 0, row + r], 1), :]
-                for k in range(1, fan_second):
-                    total = total + hidden_all[pl.ds(nbr2_ref[0, k, row + r], 1), :]
-                second_sum[pl.ds(row + r, 1), :] = total
-
-        neigh_second = (second_sum[...] / fan_second).astype(jnp.bfloat16)
-        seed_hidden = hidden_all[0:seeds, :].astype(jnp.bfloat16)
+        neigh_second = (jnp.transpose(second_t[...]) / fan_second).astype(jnp.bfloat16)
+        seed_hidden = seed_hidden_ref[...]
         w2_self = w2_pad[0]
         w2_neigh = w2_pad[1]
         logits = jnp.dot(seed_hidden, w2_self, preferred_element_type=jnp.float32) + jnp.dot(
@@ -159,26 +162,25 @@
         back_second = dot_last(grad_logits, w2_neigh) / fan_second
         back_high = back_second.astype(jnp.bfloat16)
         back_low = (back_second - back_high.astype(jnp.float32)).astype(jnp.bfloat16)
-        second_sum[...] = dot_last(grad_logits, w2_self)
-
-        grads_ref[0:at, :] = jnp.zeros((at, 128), jnp.float32)
+        seed_grad[...] = dot_last(grad_logits, w2_self)
+        grad_w1[...] = jnp.zeros_like(grad_w1)
 
         @pl.loop(0, steps)
         def _(part):
             rows = pl.ds(pl.multiple_of(part * block, block), block)
-            seen = counts_t[rows, :]
+            seen = counts_t[pl.ds(part * groups, groups)].reshape(block, seeds)
             grad = jnp.dot(seen, back_high, preferred_element_type=jnp.float32) + jnp.dot(
                 seen, back_low, preferred_element_type=jnp.float32
             )
             own = jnp.where(part == 0, 1.0, 0.0)
-            grad = grad + own * second_sum[...]
+            grad = grad + own * seed_grad[...]
             grad_pre = (grad * slope_all[rows, :]).astype(jnp.bfloat16)
-            first = dot_first(self_all[rows, :], grad_pre)
-            other = dot_first(neigh_all[rows, :], grad_pre)
-            grads_ref[0:width, :] += first[:, 0:128]
-            grads_ref[width : 2 * width, :] += first[:, 128:256]
-            grads_ref[2 * width : 3 * width, :] += other[:, 0:128]
-            grads_ref[3 * width : 4 * width, :] += other[:, 128:256]
+            grad_w1[...] += dot_first(first_all[rows, :], grad_pre)
+
+        grads_ref[0:width, :] = grad_w1[0:width, 0:128]
+        grads_ref[width : 2 * width, :] = grad_w1[0:width, 128:256]
+        grads_ref[2 * width : 3 * width, :] = grad_w1[width : 2 * width, 0:128]
+        grads_ref[3 * width : 4 * width, :] = grad_w1[width : 2 * width, 128:256]
 
 
 def sage_step(hot_rows, cold_rows, counts, mid_self, nbr1, nbr2, labels, weights):
@@ -189,7 +191,9 @@
     width, hidden = w1_self.shape
     block = seeds
     steps = middle // block
+    unit = 16
     table_rows = hot_rows.shape[0] + cold_rows.shape[0] * cold_rows.shape[1]
+    positions = nbr1.reshape(fan_first, steps, block).transpose(1, 0, 2).reshape(-1)
     vmem = pl.BlockSpec(memory_space=pltpu.VMEM)
     smem = pl.BlockSpec(memory_space=pltpu.SMEM)
     return pl.pallas_call(
@@ -201,31 +205,237 @@
         ),
         in_specs=[
             smem,
-            pl.BlockSpec((1, block), lambda i: (0, i), memory_space=pltpu.SMEM),
-            pl.BlockSpec((1, fan_first, block), lambda i: (0, 0, i), memory_space=pltpu.SMEM),
             smem,
+            pl.BlockSpec((fan_first * block,), lambda i: (i,), memory_space=pltpu.SMEM),
         ]
         + [vmem] * 8,
         out_specs=(vmem, vmem),
         scratch_shapes=[
-            pltpu.VMEM((table_rows, width), jnp.float32),
+            pltpu.VMEM((table_rows, 1, width), jnp.float32),
             pltpu.VMEM((fan_second, 8, seeds), jnp.int32),
-            pltpu.VMEM((block, width), jnp.float32),
-            pltpu.VMEM((block, width), jnp.float32),
-            pltpu.VMEM((middle, width), jnp.bfloat16),
-            pltpu.VMEM((middle, width), jnp.bfloat16),
+            pltpu.VMEM((block // unit, unit, width), jnp.float32),
+            pltpu.VMEM((block // unit, unit, width), jnp.float32),
+            pltpu.VMEM((middle, 2 * width), jnp.bfloat16),
             pltpu.VMEM((middle, hidden), jnp.float32),
-            pltpu.VMEM((middle, hidden), jnp.float32),
-            pltpu.VMEM((middle, seeds), jnp.bfloat16),
+            pltpu.VMEM((middle // unit, unit, seeds), jnp.bfloat16),
+            pltpu.VMEM((seeds, hidden), jnp.bfloat16),
+            pltpu.VMEM((hidden, seeds), jnp.float32),
             pltpu.VMEM((seeds, hidden), jnp.float32),
+            pltpu.VMEM((2 * width, hidden), jnp.bfloat16),
             pltpu.VMEM((2, hidden, 256), jnp.bfloat16),
+            pltpu.VMEM((2 * width, hidden), jnp.float32),
         ],
         compiler_params=pltpu.CompilerParams(vmem_limit_bytes=52 * 1024 * 1024),
         name="sage_step",
     )(
-        counts, mid_self, nbr1, nbr2,
+        counts, mid_self.reshape(-1), positions,
         hot_rows, cold_rows, nbr2, labels, w1_self, w1_neigh, w2_self, w2_neigh,
     )
+
+
+def fetch_kernel(
+    cliques,
+    groups,
+    hot_table,
+    cold_table,
+    hot_ids_ref,
+    cold_ids_ref,
+    hot_out,
+    cold_out,
+    hot_raw,
+    cold_raw,
+    hot_wide,
+    cold_wide,
+    hot_ask,
+    cold_ask,
+    hot_req,
+    cold_req,
+    hot_req_s,
+    cold_req_s,
+    hot_stage,
+    cold_stage,
+    hot_send,
+    cold_send,
+    local_sems,
+    hot_id_sems,
+    cold_id_sems,
+    hot_row_sems,
+    cold_row_sems,
+):
+    c = lax.axis_index("clique")
+    g = lax.axis_index("group")
+
+    def clique_at(d):
+        return (lax.rem(c + d, cliques), g)
+
+    def group_at(d):
+        return (c, lax.rem(g + d, groups))
+
+    load_cold = pltpu.make_async_copy(cold_table, cold_raw, local_sems.at[0])
+    load_hot = pltpu.make_async_copy(hot_table, hot_raw, local_sems.at[1])
+    load_cold.start()
+    load_hot.start()
+
+    barrier = pltpu.get_barrier_semaphore()
+
+    @pl.loop(1, cliques)
+    def _(d):
+        pl.semaphore_signal(barrier, inc=1, device_id=clique_at(d), device_id_type=MESH)
+
+    @pl.loop(1, groups)
+    def _(d):
+        pl.semaphore_signal(barrier, inc=1, device_id=group_at(d), device_id_type=MESH)
+
+    for j in range(cliques):
+        hot_ask[j] = hot_ids_ref[0, j : j + 1, :]
+    for o in range(groups):
+        cold_ask[o] = cold_ids_ref[0, o : o + 1, :]
+    hot_req[c] = hot_ask[c]
+    cold_req[g] = cold_ask[g]
+    pl.semaphore_wait(barrier, cliques + groups - 2)
+
+    def remote(source, target, sems, d, device):
+        return pltpu.make_async_remote_copy(
+            src_ref=source,
+            dst_ref=target,
+            send_sem=sems.at[0, d - 1],
+            recv_sem=sems.at[1, d - 1],
+            device_id=device,
+            device_id_type=MESH,
+        )
+
+    def ask_cold(d):
+        peer = lax.rem(g + d, groups)
+        return remote(cold_ask.at[peer], cold_req.at[g], cold_id_sems, d, group_at(d))
+
+    def ask_hot(d):
+        peer = lax.rem(c + d, cliques)
+        return remote(hot_ask.at[peer], hot_req.at[c], hot_id_sems, d, clique_at(d))
+
+    def give_cold(d):
+        peer = lax.rem(g + groups - d, groups)
+        return remote(
+            cold_send.at[peer], cold_out.at[g], cold_row_sems, d, group_at(groups - d)
+        )
+
+    def give_hot(d):
+        peer = lax.rem(c + cliques - d, cliques)
+        return remote(
+            hot_send.at[peer], hot_out.at[c], hot_row_sems, d, clique_at(cliques - d)
+        )
+
+    @pl.loop(1, groups)
+    def _(d):
+        ask_cold(d).start()
+
+    @pl.loop(1, cliques)
+    def _(d):
+        ask_hot(d).start()
+
+    def widen(raw, wide):
+        rows = 256
+
+        @pl.loop(0, raw.shape[0] // rows)
+        def _(part):
+            here = pl.ds(pl.multiple_of(part * rows, rows), rows)
+            wide[here, :] = raw[here, :].astype(jnp.float32)
+
+    def gather(wide, wanted, who, stage):
+        units, unit, width = stage.shape
+
+        @pl.loop(0, units)
+        def _(part):
+            for r in range(unit):
+                stage[part, r : r + 1, :] = wide[pl.ds(wanted[who, 0, part * unit + r], 1), :]
+
+        return stage[...].reshape(units * unit, width).astype(jnp.bfloat16)
+
+    load_cold.wait()
+    widen(cold_raw, cold_wide)
+
+    @pl.loop(1, groups)
+    def _(d):
+        ask_cold(d).wait()
+
+    to_scalars = pltpu.make_async_copy(cold_req, cold_req_s, local_sems.at[2])
+    to_scalars.start()
+    to_scalars.wait()
+
+    @pl.loop(1, groups)
+    def _(d):
+        peer = lax.rem(g + groups - d, groups)
+        cold_send[peer] = gather(cold_wide, cold_req_s, peer, cold_stage)
+        give_cold(d).start()
+
+    load_hot.wait()
+    widen(hot_raw, hot_wide)
+
+    @pl.loop(1, cliques)
+    def _(d):
+        ask_hot(d).wait()
+
+    to_scalars = pltpu.make_async_copy(hot_req, hot_req_s, local_sems.at[3])
+    to_scalars.start()
+    to_scalars.wait()
+
+    @pl.loop(1, cliques)
+    def _(d):
+        peer = lax.rem(c + cliques - d, cliques)
+        hot_send[peer] = gather(hot_wide, hot_req_s, peer, hot_stage)
+        give_hot(d).start()
+
+    hot_out[c] = gather(hot_wide, hot_req_s, c, hot_stage)
+    cold_out[g] = gather(cold_wide, cold_req_s, g, cold_stage)
+
+    @pl.loop(1, cliques)
+    def _(d):
+        give_hot(d).wait()
+
+    @pl.loop(1, groups)
+    def _(d):
+        give_cold(d).wait()
+
+
+def fetch_rows(hot_shard, cold_shard, hot_ids, cold_ids, cliques, groups):
+    width = hot_shard.shape[1]
+    hot_slots, cold_slots = hot_ids.shape[2], cold_ids.shape[2]
+    vmem = pl.BlockSpec(memory_space=pltpu.VMEM)
+    anywhere = pl.BlockSpec(memory_space=pl.ANY)
+    bf16, f32, i32 = jnp.bfloat16, jnp.float32, jnp.int32
+    return pl.pallas_call(
+        partial(fetch_kernel, cliques, groups),
+        out_shape=(
+            jax.ShapeDtypeStruct((cliques, hot_slots, width), bf16),
+            jax.ShapeDtypeStruct((groups, cold_slots, width), bf16),
+        ),
+        in_specs=[anywhere, anywhere, vmem, vmem],
+        out_specs=(vmem, vmem),
+        scratch_shapes=[
+            pltpu.VMEM(hot_shard.shape, bf16),
+            pltpu.VMEM(cold_shard.shape, bf16),
+            pltpu.VMEM(hot_shard.shape, f32),
+            pltpu.VMEM(cold_shard.shape, f32),
+            pltpu.VMEM((cliques, 1, hot_slots), i32),
+            pltpu.VMEM((groups, 1, cold_slots), i32),
+            pltpu.VMEM((cliques, 1, hot_slots), i32),
+            pltpu.VMEM((groups, 1, cold_slots), i32),
+            pltpu.SMEM((cliques, 1, hot_slots), i32),
+            pltpu.SMEM((groups, 1, cold_slots), i32),
+            pltpu.VMEM((hot_slots // 16, 16, width), f32),
+            pltpu.VMEM((cold_slots // 16, 16, width), f32),
+            pltpu.VMEM((cliques, hot_slots, width), bf16),
+            pltpu.VMEM((groups, cold_slots, width), bf16),
+            pltpu.SemaphoreType.DMA((4,)),
+            pltpu.SemaphoreType.DMA((2, cliques - 1)),
+            pltpu.SemaphoreType.DMA((2, groups - 1)),
+            pltpu.SemaphoreType.DMA((2, cliques - 1)),
+            pltpu.SemaphoreType.DMA((2, groups - 1)),
+        ],
+        compiler_params=pltpu.CompilerParams(
+            collective_id=1, has_side_effects=True, vmem_limit_bytes=48 * 1024 * 1024
+        ),
+        name="fetch_rows",
+    )(hot_shard, cold_shard, hot_ids, cold_ids)
 
 
 def reduce_kernel(
@@ -408,25 +618,9 @@
     w2_self,
     w2_neigh,
 ):
-    width = hot_shard.shape[1]
-    requests = lax.all_to_all(hot_ids[0], "clique", split_axis=0, concat_axis=0, tiled=True)
-    served = jnp.take(hot_shard, requests, axis=0)
-    hot_rows = lax.all_to_all(served, "clique", split_axis=0, concat_axis=0, tiled=True).reshape(
-        -1, width
-    )
-    fetched = lax.all_to_all(
-        jnp.take(
-            cold_shard,
-            lax.all_to_all(cold_ids[0], "group", split_axis=0, concat_axis=0, tiled=True),
-            axis=0,
-        ),
-        "group",
-        split_axis=0,
-        concat_axis=0,
-        tiled=True,
-    )
+    hot_rows, cold_rows = fetch_rows(hot_shard, cold_shard, hot_ids, cold_ids, cliques, groups)
     seed_loss, terms = sage_step(
-        hot_rows, fetched, cold_counts, mid_self, nbr1, nbr2, labels,
+        hot_rows.reshape(-1, hot_shard.shape[1]), cold_rows, cold_counts, mid_self, nbr1, nbr2, labels,
         (w1_self, w1_neigh, w2_self, w2_neigh),
     )
     shapes = (w1_self.shape, w1_neigh.shape, w2_self.shape, w2_neigh.shape)

time: 244 us -> 160 us (0.66)
  Pallas kernels: 179 us -> 146 us
  starting transfers between devices: 18.8 us -> 0 us
  waiting for transfers between devices: 18.4 us -> 0 us
  local copies, waits for them, and re-layouts: 23.5 us -> 10.6 us
    pallas_call x1, Pallas kernels: 155 us -> 96.3 us  [sage_step(): pl.pallas_call(sage_kernel, grid=(steps,), out_shape=(jax.ShapeDtypeStruc...]
    pallas_call x0 -> x1, Pallas kernels: none -> 26.1 us  [fetch_rows(): pl.pallas_call(partial(fetch_kernel, cliques, groups), out_shape=(jax.Sha...]
    all_to_all x4 -> x0, starting transfers between devices: 18.8 us -> none  [the longest x1 5.16 us: body(): lax.all_to_all(hot_ids[0], 'clique', split_axis=0, concat_axis=0, tiled=T...]
    all_to_all x4 -> x0, waiting for transfers between devices: 18.4 us -> none  [the longest x1 15 us: body(): lax.all_to_all(jnp.take(cold_shard, lax.all_to_all(cold_ids[0], 'group',...]
    gather x2 -> x0, local copies, waits for them, and re-layouts: 16.7 us -> none  [the longest x1 8.35 us: body(): jnp.take(cold_shard, lax.all_to_all(cold_ids[0], 'group', split_axis=0, c...]
    unnamed x28 -> x23, local copies, waits for them, and re-layouts: 4.26 us -> 10.3 us
    all_to_all x2 -> x0, local copies, waits for them, and re-layouts: 2.6 us -> none  [the longest x1 1.3 us: body(): lax.all_to_all(hot_ids[0], 'clique', split_axis=0, concat_axis=0, tiled=T...]
    unnamed x0 -> x2, other arithmetic: none -> 2.54 us
  transfers between devices with their start and end apart: 4 -> 0, of which waited for: 2 -> 0; matrix products, arithmetic and copies ran while one was open for 8% -> 0% of each run, Pallas kernels for 0% -> 0%
where the time goes in v2:
time: 160 us
  Pallas kernels  146 us (91%)
  local copies, waits for them, and re-layouts  10.6 us (7%)
  other arithmetic  2.54 us (2%)
    pallas_call x1, Pallas kernels, sage_step(): pl.pallas_call(sage_kernel, grid=(steps,), out_shape=(jax.ShapeDtypeStruc...  96.3 us
    pallas_call x1, Pallas kernels, fetch_rows(): pl.pallas_call(partial(fetch_kernel, cliques, groups), out_shape=(jax.Sha...  26.1 us
    pallas_call x1, Pallas kernels, reduce_terms(): pl.pallas_call(partial(reduce_kernel, cliques, groups), out_shape=tuple((...  23.2 us
    unnamed x23, local copies, waits for them, and re-layouts  10.3 us

profile of v2, /device:TPU:0, one launch (start us, length us, event | category | flops | bytes accessed | tf_op | source)
XLA Modules:
  0.0 159.6 jit_solution(5980395790003410186)
XLA Ops:
  0.6 0.8 reduce.self_ref
  1.5 0.8 copy.24.nbr2_ref
  2.2 1.0 copy.25.w2_self_ref
  3.2 1.0 copy.26.w2_neigh_ref
  4.2 1.7 %reduce.1 = s32[10,7680]{1,0:T(8,128)S(1)} reduce(s32[1,10,7680]{2,0,1:T(1,128)} %param.19, s32[]{:T(128)} %constant.7), dimensions={0}, to_apply=%param.19.reduce_sub_computation | reduce | bytes 614404 | tf_op args[6]
  5.9 0.1 reshape.23
  6.1 0.2 copy.30
  6.3 0.0 copy-start
  6.3 2.2 %copy-done = bf16[16384,128]{1,0:T(8,128)(2,1)S(1)} copy-done((bf16[16384,128]{1,0:T(8,128)(2,1)S(1)}, bf16[16384,128]{1,0:T(8,128)(2,1)}, u32[]{:S(2)}) %copy-start) | copy-done | bytes 4194328
  8.5 0.0 copy-start.4
  8.5 0.7 copy-done.4
  9.2 0.0 copy-start.5
  9.2 0.7 copy-done.5
  9.9 0.0 copy-start.2
  9.9 0.0 copy-start.3
  9.9 0.0 copy-start.6
  9.9 0.0 copy-start.7
  9.9 26.1 %fetch_rows.1 = (bf16[4,512,128]{2,1,0:T(8,128)(2,1)S(1)}, bf16[8,256,128]{2,1,0:T(8,128)(2,1)S(1)}) custom-call(bf16[16384,128]{1,0:T(8,128)(2,1)S(1)} %copy-done, bf16[16384,128]{1,0:T(8,128)(2,1)} %cold_table.1, s32[1,4,512]{2,1,0:T(4,128)S(1)} %copy-done.4, s32[1,8,256]{2,1,0:T(8,128)S(1)} %copy-done.5), custom_call_target="tpu_custom_call" | custom-call | tf_op jit(solution)/shard_map/fetch_rows/pallas_call | solution.py:405
  36.0 0.0 copy-done.2
  36.1 0.0 copy-done.3
  36.1 0.0 copy-done.6
  36.1 0.0 copy-done.7
  36.1 96.3 %sage_step.1 = (f32[1,512]{1,0:T(1,128)}, f32[1280,128]{1,0:T(8,128)}) custom-call(s32[1,8]{1,0:T(1,128)S(1)} %copy-done.7, s32[7680]{0:T(1024)S(1)} %reduce.self_ref, s32[76800]{0:T(1024)S(1)} %reshape.24.nbr1_ref, bf16[2048,128]{1,0:T(8,128)(2,1)S(1)} %bitcast.4, bf16[8,256,128]{2,1,0:T(8,128)(2,1)S(1)} %get-tuple-element.14.cold_ref, ...), custom_call_target="tpu_custom_call" | custom-call | tf_op jit(solution)/shard_map/sage_step/pallas_call | solution.py:199
  132.4 0.0 copy-start.1
  132.4 1.1 copy-done.1
  133.4 23.2 %reduce_terms.1 = (f32[128,256]{1,0:T(8,128)S(1)}, f32[128,256]{1,0:T(8,128)S(1)}, f32[256,172]{1,0:T(8,128)S(1)}, f32[256,172]{1,0:T(8,128)S(1)}) custom-call(f32[1280,128]{1,0:T(8,128)S(1)} %copy-done.1), custom_call_target="tpu_custom_call" | custom-call | tf_op jit(solution)/shard_map/reduce_terms/pallas_call | solution.py:581
  156.7 0.8 copy.27
  157.5 0.8 copy.28
  158.2 0.7 copy.33
  158.9 0.7 copy.34
  (1 shorter events, 0.0 us)
Async XLA Ops:
  6.3 2.2 %copy-start = (bf16[16384,128]{1,0:T(8,128)(2,1)S(1)}, bf16[16384,128]{1,0:T(8,128)(2,1)}, u32[]{:S(2)}) copy-start(bf16[16384,128]{1,0:T(8,128)(2,1)} %hot_table.1) | copy-start | bytes 12582916
  8.5 0.7 copy-start.4
  9.2 0.7 copy-start.5
  9.9 26.2 %copy-start.2 = (bf16[128,256]{1,0:T(8,128)(2,1)S(1)}, bf16[128,256]{1,0:T(8,128)(2,1)}, u32[]{:S(2)}) copy-start(bf16[128,256]{1,0:T(8,128)(2,1)} %w1_self_ref.1) | copy-start | bytes 196612
  9.9 26.2 %copy-start.3 = (bf16[128,256]{1,0:T(8,128)(2,1)S(1)}, bf16[128,256]{1,0:T(8,128)(2,1)}, u32[]{:S(2)}) copy-start(bf16[128,256]{1,0:T(8,128)(2,1)} %w1_neigh_ref.1) | copy-start | bytes 196612
  9.9 26.2 %copy-start.6 = (s32[1,512]{1,0:T(1,128)S(1)}, s32[1,512]{1,0:T(1,128)}, u32[]{:S(2)}) copy-start(s32[1,512]{1,0:T(1,128)} %labels_ref.1) | copy-start | bytes 6148
  9.9 26.2 %copy-start.7 = (s32[1,8]{1,0:T(1,128)S(1)}, s32[1,8]{1,0:T(1,128)}, u32[]{:S(2)}) copy-start(s32[1,8]{1,0:T(1,128)} %counts_ref.1) | copy-start | bytes 100
  132.4 1.1 copy-start.1

commit v3 on v2

--- a/solution.py
+++ b/solution.py
@@ -41,12 +41,14 @@
     grads_ref,
     table,
     spread_ids,
-    self_rows,
-    sum_rows,
+    self_even,
+    sum_even,
+    self_odd,
+    sum_odd,
     first_all,
     slope_all,
+    hidden_all,
     counts_t,
-    seed_hidden_ref,
     second_t,
     seed_grad,
     w1_both,
@@ -55,15 +57,19 @@
 ):
     step = pl.program_id(0)
     steps = pl.num_programs(0)
-    groups, unit, width = sum_rows.shape
-    block = groups * unit
+    units, unit, width = sum_even.shape
+    part_rows = units * unit
+    middle = first_all.shape[0]
+    block = middle // steps
+    pairs = block // (2 * part_rows)
     fan_first = nbr1_ref.shape[0] // block
     fan_second, seeds = nbr2_ref.shape[1], nbr2_ref.shape[2]
     owners, slots, _ = cold_ref.shape
     hot_rows = hot_ref.shape[0]
     hidden = w1_self_ref.shape[1]
-    classes = w2_self_ref.shape[1]
-    padded = w2_pad.shape[2]
+    classes = w2_self_ref.shape[0]
+    padded = w2_pad.shape[1]
+    count_type = spread_ids.dtype
 
     @pl.when(step == 0)
     def _():
@@ -81,63 +87,76 @@
                 table[hot_rows + owner * slots + r] = rows[r : r + 1, :]
 
         for k in range(fan_second):
-            spread_ids[k] = jnp.broadcast_to(nbr2_ref[0, k : k + 1, :], (8, seeds))
+            spread_ids[k] = jnp.broadcast_to(nbr2_ref[0, k : k + 1, :], (unit, seeds)).astype(
+                count_type
+            )
         w1_both[0:width, :] = w1_self_ref[...]
         w1_both[width : 2 * width, :] = w1_neigh_ref[...]
         w2_pad[...] = jnp.zeros_like(w2_pad)
-        w2_pad[0, :, 0:classes] = w2_self_ref[...]
-        w2_pad[1, :, 0:classes] = w2_neigh_ref[...]
-        second_t[...] = jnp.zeros_like(second_t)
-
-    node_base = step * block
-
-    @pl.loop(0, groups)
-    def _(group):
-        row = group * unit
-        for r in range(unit):
-            total = table[nbr1_ref[row + r]]
-            for k in range(1, fan_first):
-                total = total + table[nbr1_ref[row + (k * block + r)]]
-            sum_rows[group, r : r + 1, :] = total
-            self_rows[group, r : r + 1, :] = table[self_ref[node_base + row + r]]
-        halves = []
-        for half in range(unit // 8):
-            node = lax.broadcasted_iota(jnp.int32, (8, seeds), 0) + (node_base + row + half * 8)
-            seen = jnp.zeros((8, seeds), jnp.float32)
+        w2_pad[0, 0:classes, :] = w2_self_ref[...]
+        w2_pad[1, 0:classes, :] = w2_neigh_ref[...]
+        self_odd[...] = jnp.zeros_like(self_odd)
+        sum_odd[...] = jnp.zeros_like(sum_odd)
+
+    def gather(local, start, self_rows, sum_rows):
+        for u in range(units):
+            for r in range(unit):
+                at = u * unit + r
+                total = table[nbr1_ref[local + at]]
+                for k in range(1, fan_first):
+                    total = total + table[nbr1_ref[local + (k * block + at)]]
+                sum_rows[u, r : r + 1, :] = total
+                self_rows[u, r : r + 1, :] = table[self_ref[start + at]]
+            node = (
+                lax.broadcasted_iota(jnp.int32, (unit, seeds), 0) + (start + u * unit)
+            ).astype(count_type)
+            seen = jnp.zeros((unit, seeds), jnp.bfloat16)
+            one = jnp.ones((unit, seeds), jnp.bfloat16)
+            none = jnp.zeros((unit, seeds), jnp.bfloat16)
             for k in range(fan_second):
-                seen = seen + jnp.where(spread_ids[k] == node, 1.0, 0.0)
-            halves.append(seen)
-        counts_t[step * groups + group] = jnp.concatenate(halves, axis=0).astype(jnp.bfloat16)
-
-    here = pl.ds(pl.multiple_of(node_base, block), block)
-    self_first = self_rows[...].reshape(block, width).astype(jnp.bfloat16)
-    neigh_first = (sum_rows[...].reshape(block, width) / fan_first).astype(jnp.bfloat16)
-    first = jnp.concatenate([self_first, neigh_first], axis=1)
-    first_all[here, :] = first
-    pre = jnp.dot(first, w1_both[...], preferred_element_type=jnp.float32)
-    square = pre * pre
-    bend = jnp.tanh(GELU_SCALE * (pre + GELU_CUBE * (square * pre)))
-    half_up = 0.5 * (1.0 + bend)
-    hidden_first = (pre * half_up).astype(jnp.bfloat16)
-    slope_all[here, :] = half_up + (0.5 * GELU_SCALE) * pre * (1.0 - bend * bend) * (
-        1.0 + (3.0 * GELU_CUBE) * square
-    )
-    seen = counts_t[pl.ds(step * groups, groups)].reshape(block, seeds)
-    second_t[...] += dot_first(hidden_first, seen)
-
-    @pl.when(step == 0)
-    def _():
-        seed_hidden_ref[...] = hidden_first
+                seen = seen + jnp.where(spread_ids[k] == node, one, none)
+            counts_t[start // unit + u] = seen
+
+    def dense(start, self_rows, sum_rows):
+        here = pl.ds(pl.multiple_of(start, part_rows), part_rows)
+        self_first = self_rows[...].reshape(part_rows, width).astype(jnp.bfloat16)
+        neigh_first = (sum_rows[...].reshape(part_rows, width) / fan_first).astype(jnp.bfloat16)
+        first = jnp.concatenate([self_first, neigh_first], axis=1)
+        first_all[here, :] = first
+        pre = jnp.dot(first, w1_both[...], preferred_element_type=jnp.float32)
+        square = pre * pre
+        bend = jnp.tanh(GELU_SCALE * (pre + GELU_CUBE * (square * pre)))
+        half_up = 0.5 * (1.0 + bend)
+        hidden_all[here, :] = (pre * half_up).astype(jnp.bfloat16)
+        slope_all[here, :] = half_up + (0.5 * GELU_SCALE) * pre * (1.0 - bend * bend) * (
+            1.0 + (3.0 * GELU_CUBE) * square
+        )
+
+    @pl.loop(0, pairs)
+    def _(pair):
+        local = pair * (2 * part_rows)
+        start = step * block + local
+        gather(local, start, self_even, sum_even)
+        dense(jnp.maximum(start - part_rows, part_rows), self_odd, sum_odd)
+        gather(local + part_rows, start + part_rows, self_odd, sum_odd)
+        dense(start, self_even, sum_even)
 
     @pl.when(step == steps - 1)
     def _():
+        dense(middle - part_rows, self_odd, sum_odd)
+        second_t[...] = jnp.zeros_like(second_t)
+
+        @pl.loop(0, steps)
+        def _(part):
+            rows = pl.ds(pl.multiple_of(part * block, block), block)
+            seen = counts_t[pl.ds(part * (block // unit), block // unit)].reshape(block, seeds)
+            second_t[...] += dot_first(hidden_all[rows, :], seen)
+
         neigh_second = (jnp.transpose(second_t[...]) / fan_second).astype(jnp.bfloat16)
-        seed_hidden = seed_hidden_ref[...]
+        seed_hidden = hidden_all[0:seeds, :]
         w2_self = w2_pad[0]
         w2_neigh = w2_pad[1]
-        logits = jnp.dot(seed_hidden, w2_self, preferred_element_type=jnp.float32) + jnp.dot(
-            neigh_second, w2_neigh, preferred_element_type=jnp.float32
-        )
+        logits = dot_last(seed_hidden, w2_self) + dot_last(neigh_second, w2_neigh)
         column = lax.broadcasted_iota(jnp.int32, (seeds, padded), 1)
         real = column < classes
         log_total = jnp.log(
@@ -151,24 +170,29 @@
         loss_ref[...] = jnp.transpose(loss)[0:1, :]
         probs = jnp.where(real, jnp.exp(logits - log_total), 0.0)
         grad_logits = ((probs - onehot) / seeds).astype(jnp.bfloat16)
-        term_self = dot_first(seed_hidden, grad_logits)
-        term_neigh = dot_first(neigh_second, grad_logits)
+        term_self = dot_first(grad_logits, seed_hidden)
+        term_neigh = dot_first(grad_logits, neigh_second)
         at = 4 * width
-        grads_ref[at : at + hidden, :] = term_self[:, 0:128]
-        grads_ref[at + hidden : at + 2 * hidden, :] = term_neigh[:, 0:128]
-        grads_ref[at + 2 * hidden : at + 3 * hidden, :] = term_self[:, 128:256] + pltpu.roll(
-            term_neigh[:, 128:256], 64, 1
-        )
-        back_second = dot_last(grad_logits, w2_neigh) / fan_second
+        high = -(-classes // 8) * 8
+        grads_ref[at : at + high, :] = term_self[0:high, 0:128]
+        grads_ref[at + high : at + 2 * high, :] = term_self[0:high, 128:256]
+        grads_ref[at + 2 * high : at + 3 * high, :] = term_neigh[0:high, 0:128]
+        grads_ref[at + 3 * high : at + 4 * high, :] = term_neigh[0:high, 128:256]
+        rest = grads_ref.shape[0] - (at + 4 * high)
+        if rest > 0:
+            grads_ref[at + 4 * high :, :] = jnp.zeros((rest, 128), jnp.float32)
+        back_second = (
+            jnp.dot(grad_logits, w2_neigh, preferred_element_type=jnp.float32) / fan_second
+        )
         back_high = back_second.astype(jnp.bfloat16)
         back_low = (back_second - back_high.astype(jnp.float32)).astype(jnp.bfloat16)
-        seed_grad[...] = dot_last(grad_logits, w2_self)
+        seed_grad[...] = jnp.dot(grad_logits, w2_self, preferred_element_type=jnp.float32)
         grad_w1[...] = jnp.zeros_like(grad_w1)
 
-        @pl.loop(0, steps)
+        @pl.loop(0, middle // seeds)
         def _(part):
-            rows = pl.ds(pl.multiple_of(part * block, block), block)
-            seen = counts_t[pl.ds(part * groups, groups)].reshape(block, seeds)
+            rows = pl.ds(pl.multiple_of(part * seeds, seeds), seeds)
+            seen = counts_t[pl.ds(part * (seeds // unit), seeds // unit)].reshape(seeds, seeds)
             grad = jnp.dot(seen, back_high, preferred_element_type=jnp.float32) + jnp.dot(
                 seen, back_low, preferred_element_type=jnp.float32
             )
@@ -189,13 +213,14 @@
     middle = mid_self.shape[1]
     fan_first, fan_second = nbr1.shape[1], nbr2.shape[1]
     width, hidden = w1_self.shape
-    block = seeds
+    block = 3 * seeds
     steps = middle // block
-    unit = 16
+    unit, units = 16, 4
     table_rows = hot_rows.shape[0] + cold_rows.shape[0] * cold_rows.shape[1]
     positions = nbr1.reshape(fan_first, steps, block).transpose(1, 0, 2).reshape(-1)
     vmem = pl.BlockSpec(memory_space=pltpu.VMEM)
     smem = pl.BlockSpec(memory_space=pltpu.SMEM)
+    rows_buffer = pltpu.VMEM((units, unit, width), jnp.float32)
     return pl.pallas_call(
         sage_kernel,
         grid=(steps,),
@@ -212,24 +237,26 @@
         out_specs=(vmem, vmem),
         scratch_shapes=[
             pltpu.VMEM((table_rows, 1, width), jnp.float32),
-            pltpu.VMEM((fan_second, 8, seeds), jnp.int32),
-            pltpu.VMEM((block // unit, unit, width), jnp.float32),
-            pltpu.VMEM((block // unit, unit, width), jnp.float32),
+            pltpu.VMEM((fan_second, unit, seeds), jnp.int16),
+            rows_buffer,
+            rows_buffer,
+            rows_buffer,
+            rows_buffer,
             pltpu.VMEM((middle, 2 * width), jnp.bfloat16),
             pltpu.VMEM((middle, hidden), jnp.float32),
+            pltpu.VMEM((middle, hidden), jnp.bfloat16),
             pltpu.VMEM((middle // unit, unit, seeds), jnp.bfloat16),
-            pltpu.VMEM((seeds, hidden), jnp.bfloat16),
             pltpu.VMEM((hidden, seeds), jnp.float32),
             pltpu.VMEM((seeds, hidden), jnp.float32),
             pltpu.VMEM((2 * width, hidden), jnp.bfloat16),
-            pltpu.VMEM((2, hidden, 256), jnp.bfloat16),
+            pltpu.VMEM((2, 256, hidden), jnp.bfloat16),
             pltpu.VMEM((2 * width, hidden), jnp.float32),
         ],
         compiler_params=pltpu.CompilerParams(vmem_limit_bytes=52 * 1024 * 1024),
         name="sage_step",
     )(
         counts, mid_self.reshape(-1), positions,
-        hot_rows, cold_rows, nbr2, labels, w1_self, w1_neigh, w2_self, w2_neigh,
+        hot_rows, cold_rows, nbr2, labels, w1_self, w1_neigh, w2_self.T, w2_neigh.T,
     )
 
 
@@ -559,17 +586,17 @@
     copy.wait()
 
     width, hidden = w1_self_ref.shape
-    tail = w2_self_ref.shape[1] - 128
+    classes = w2_self_ref.shape[0]
+    high = -(-classes // 8) * 8
     w1_self_ref[:, 0:128] = back[0:width, :]
     w1_self_ref[:, 128:256] = back[width : 2 * width, :]
     w1_neigh_ref[:, 0:128] = back[2 * width : 3 * width, :]
     w1_neigh_ref[:, 128:256] = back[3 * width : 4 * width, :]
     at = 4 * width
-    w2_self_ref[:, 0:128] = back[at : at + hidden, :]
-    w2_neigh_ref[:, 0:128] = back[at + hidden : at + 2 * hidden, :]
-    tails = back[at + 2 * hidden : at + 3 * hidden, :]
-    w2_self_ref[:, 128 : 128 + tail] = tails[:, 0:tail]
-    w2_neigh_ref[:, 128 : 128 + tail] = pltpu.roll(tails, 64, 1)[:, 0:tail]
+    w2_self_ref[:, 0:128] = back[at : at + classes, :]
+    w2_self_ref[:, 128:256] = back[at + high : at + high + classes, :]
+    w2_neigh_ref[:, 0:128] = back[at + 2 * high : at + 2 * high + classes, :]
+    w2_neigh_ref[:, 128:256] = back[at + 3 * high : at + 3 * high + classes, :]
 
 
 def reduce_terms(terms, shapes, cliques, groups):
@@ -623,9 +650,9 @@
         hot_rows.reshape(-1, hot_shard.shape[1]), cold_rows, cold_counts, mid_self, nbr1, nbr2, labels,
         (w1_self, w1_neigh, w2_self, w2_neigh),
     )
-    shapes = (w1_self.shape, w1_neigh.shape, w2_self.shape, w2_neigh.shape)
+    shapes = (w1_self.shape, w1_neigh.shape, w2_self.T.shape, w2_neigh.T.shape)
     totals = reduce_terms(terms, shapes, cliques, groups)
-    return (seed_loss, totals[0], totals[1], totals[2], totals[3])
+    return (seed_loss, totals[0], totals[1], totals[2].T, totals[3].T)
 
 
 def solution(mesh):

time: 160 us -> 152 us (0.950)
  Pallas kernels: 146 us -> 140 us
  local copies, waits for them, and re-layouts: 10.6 us -> 8.49 us
    pallas_call x1, Pallas kernels: 96.3 us -> 90.5 us  [sage_step(): pl.pallas_call(sage_kernel, grid=(steps,), out_shape=(jax.ShapeDtypeStruc...]
    unnamed x23 -> x25, local copies, waits for them, and re-layouts: 10.3 us -> 8.1 us
where the time goes in v3:
time: 152 us
  Pallas kernels  140 us (92%)
  local copies, waits for them, and re-layouts  8.49 us (6%)
  other arithmetic  2.54 us (2%)
    pallas_call x1, Pallas kernels, sage_step(): pl.pallas_call(sage_kernel, grid=(steps,), out_shape=(jax.ShapeDtypeStruc...  90.5 us
    pallas_call x1, Pallas kernels, fetch_rows(): pl.pallas_call(partial(fetch_kernel, cliques, groups), out_shape=(jax.Sha...  26.1 us
    pallas_call x1, Pallas kernels, reduce_terms(): pl.pallas_call(partial(reduce_kernel, cliques, groups), out_shape=tuple((...  23.1 us
    unnamed x25, local copies, waits for them, and re-layouts  8.1 us

profile of v3, /device:TPU:0, one launch (start us, length us, event | category | flops | bytes accessed | tf_op | source)
XLA Modules:
  0.0 151.6 jit_solution(15454526778047527423)
XLA Ops:
  0.6 0.8 reduce.self_ref
  1.5 0.8 copy.20.nbr2_ref
  2.2 1.7 %reduce.1 = s32[10,7680]{1,0:T(8,128)S(1)} reduce(s32[1,10,7680]{2,0,1:T(1,128)} %param.19, s32[]{:T(128)} %constant.7), dimensions={0}, to_apply=%param.19.reduce_sub_computation | reduce | bytes 614404 | tf_op args[6]
  3.9 0.2 reshape.23
  4.1 0.2 copy.22
  4.3 0.0 copy-start
  4.4 2.2 %copy-done = bf16[16384,128]{1,0:T(8,128)(2,1)S(1)} copy-done((bf16[16384,128]{1,0:T(8,128)(2,1)S(1)}, bf16[16384,128]{1,0:T(8,128)(2,1)}, u32[]{:S(2)}) %copy-start) | copy-done | bytes 4194328
  6.5 0.0 copy-start.6
  6.5 0.7 copy-done.6
  7.2 0.0 copy-start.7
  7.2 0.7 copy-done.7
  7.9 0.0 copy-start.2
  7.9 0.0 copy-start.3
  7.9 0.0 copy-start.4
  7.9 0.0 copy-start.5
  7.9 0.0 copy-start.8
  8.0 0.0 copy-start.9
  8.0 26.1 %fetch_rows.1 = (bf16[4,512,128]{2,1,0:T(8,128)(2,1)S(1)}, bf16[8,256,128]{2,1,0:T(8,128)(2,1)S(1)}) custom-call(bf16[16384,128]{1,0:T(8,128)(2,1)S(1)} %copy-done, bf16[16384,128]{1,0:T(8,128)(2,1)} %cold_table.1, s32[1,4,512]{2,1,0:T(4,128)S(1)} %copy-done.6, s32[1,8,256]{2,1,0:T(8,128)S(1)} %copy-done.7), custom_call_target="tpu_custom_call" | custom-call | tf_op jit(solution)/shard_map/fetch_rows/pallas_call | solution.py:432
  34.1 0.0 copy-done.2
  34.1 0.0 copy-done.3
  34.1 0.0 copy-done.4
  34.1 0.0 copy-done.5
  34.1 0.0 copy-done.8
  34.2 0.0 copy-done.9
  34.2 90.5 %sage_step.1 = (f32[1,512]{1,0:T(1,128)}, f32[1280,128]{1,0:T(8,128)}) custom-call(s32[1,8]{1,0:T(1,128)S(1)} %copy-done.9, s32[7680]{0:T(1024)S(1)} %reduce.self_ref, s32[76800]{0:T(1024)S(1)} %reshape.24.nbr1_ref, bf16[2048,128]{1,0:T(8,128)(2,1)S(1)} %bitcast.8, bf16[8,256,128]{2,1,0:T(8,128)(2,1)S(1)} %get-tuple-element.14.cold_ref, ...), custom_call_target="tpu_custom_call" | custom-call | tf_op jit(solution)/shard_map/sage_step/pallas_call | solution.py:224
  124.7 0.0 copy-start.1
  124.7 1.1 copy-done.1
  125.8 23.1 %reduce_terms.1 = (f32[128,256]{1,0:T(8,128)S(1)}, f32[128,256]{1,0:T(8,128)S(1)}, f32[172,256]{1,0:T(8,128)S(1)}, f32[172,256]{1,0:T(8,128)S(1)}) custom-call(f32[1280,128]{1,0:T(8,128)S(1)} %copy-done.1), custom_call_target="tpu_custom_call" | custom-call | tf_op jit(solution)/shard_map/reduce_terms/pallas_call | solution.py:608
  148.9 0.7 copy.27
  149.6 0.7 copy.28
  150.2 0.7 copy.29
  150.9 0.7 copy.30
  (1 shorter events, 0.0 us)
Async XLA Ops:
  4.3 2.2 %copy-start = (bf16[16384,128]{1,0:T(8,128)(2,1)S(1)}, bf16[16384,128]{1,0:T(8,128)(2,1)}, u32[]{:S(2)}) copy-start(bf16[16384,128]{1,0:T(8,128)(2,1)} %hot_table.1) | copy-start | bytes 12582916
  6.5 0.7 copy-start.6
  7.2 0.7 copy-start.7
  7.9 26.2 %copy-start.2 = (bf16[256,172]{0,1:T(8,128)(2,1)S(1)}, bf16[256,172]{0,1:T(8,128)(2,1)}, u32[]{:S(2)}) copy-start(bf16[256,172]{0,1:T(8,128)(2,1)} %param.24) | copy-start | bytes 264196
  7.9 26.2 %copy-start.3 = (bf16[256,172]{0,1:T(8,128)(2,1)S(1)}, bf16[256,172]{0,1:T(8,128)(2,1)}, u32[]{:S(2)}) copy-start(bf16[256,172]{0,1:T(8,128)(2,1)} %param.25) | copy-start | bytes 264196
  7.9 26.2 %copy-start.4 = (bf16[128,256]{1,0:T(8,128)(2,1)S(1)}, bf16[128,256]{1,0:T(8,128)(2,1)}, u32[]{:S(2)}) copy-start(bf16[128,256]{1,0:T(8,128)(2,1)} %w1_self_ref.1) | copy-start | bytes 196612
  7.9 26.2 %copy-start.5 = (bf16[128,256]{1,0:T(8,128)(2,1)S(1)}, bf16[128,256]{1,0:T(8,128)(2,1)}, u32[]{:S(2)}) copy-start(bf16[128,256]{1,0:T(8,128)(2,1)} %w1_neigh_ref.1) | copy-start | bytes 196612
  7.9 26.2 %copy-start.8 = (s32[1,512]{1,0:T(1,128)S(1)}, s32[1,512]{1,0:T(1,128)}, u32[]{:S(2)}) copy-start(s32[1,512]{1,0:T(1,128)} %labels_ref.1) | copy-start | bytes 6148
  8.0 26.2 %copy-start.9 = (s32[1,8]{1,0:T(1,128)S(1)}, s32[1,8]{1,0:T(1,128)}, u32[]{:S(2)}) copy-start(s32[1,8]{1,0:T(1,128)} %counts_ref.1) | copy-start | bytes 100
  124.7 1.1 copy-start.1

commit v4 on v3

--- a/solution.py
+++ b/solution.py
@@ -62,8 +62,8 @@
     middle = first_all.shape[0]
     block = middle // steps
     pairs = block // (2 * part_rows)
-    fan_first = nbr1_ref.shape[0] // block
-    fan_second, seeds = nbr2_ref.shape[1], nbr2_ref.shape[2]
+    fan_first = nbr1_ref.shape[0]
+    fan_second, seeds = nbr2_ref.shape[0], nbr2_ref.shape[2]
     owners, slots, _ = cold_ref.shape
     hot_rows = hot_ref.shape[0]
     hidden = w1_self_ref.shape[1]
@@ -87,7 +87,7 @@
                 table[hot_rows + owner * slots + r] = rows[r : r + 1, :]
 
         for k in range(fan_second):
-            spread_ids[k] = jnp.broadcast_to(nbr2_ref[0, k : k + 1, :], (unit, seeds)).astype(
+            spread_ids[k] = jnp.broadcast_to(nbr2_ref[k], (unit, seeds)).astype(
                 count_type
             )
         w1_both[0:width, :] = w1_self_ref[...]
@@ -98,15 +98,15 @@
         self_odd[...] = jnp.zeros_like(self_odd)
         sum_odd[...] = jnp.zeros_like(sum_odd)
 
-    def gather(local, start, self_rows, sum_rows):
+    def gather(near, own, offset, start, self_rows, sum_rows):
         for u in range(units):
             for r in range(unit):
-                at = u * unit + r
-                total = table[nbr1_ref[local + at]]
+                at = offset + u * unit + r
+                total = table[near[0][at]]
                 for k in range(1, fan_first):
-                    total = total + table[nbr1_ref[local + (k * block + at)]]
+                    total = total + table[near[k][at]]
                 sum_rows[u, r : r + 1, :] = total
-                self_rows[u, r : r + 1, :] = table[self_ref[start + at]]
+                self_rows[u, r : r + 1, :] = table[own[at]]
             node = (
                 lax.broadcasted_iota(jnp.int32, (unit, seeds), 0) + (start + u * unit)
             ).astype(count_type)
@@ -134,11 +134,14 @@
 
     @pl.loop(0, pairs)
     def _(pair):
-        local = pair * (2 * part_rows)
-        start = step * block + local
-        gather(local, start, self_even, sum_even)
+        span = 2 * part_rows
+        local = pl.multiple_of(pair * span, span)
+        start = pl.multiple_of(step * block + local, span)
+        near = [nbr1_ref.at[k, 0, pl.ds(local, span)] for k in range(fan_first)]
+        own = self_ref.at[0, pl.ds(start, span)]
+        gather(near, own, 0, start, self_even, sum_even)
         dense(jnp.maximum(start - part_rows, part_rows), self_odd, sum_odd)
-        gather(local + part_rows, start + part_rows, self_odd, sum_odd)
+        gather(near, own, part_rows, start + part_rows, self_odd, sum_odd)
         dense(start, self_even, sum_even)
 
     @pl.when(step == steps - 1)
@@ -189,7 +192,7 @@
         seed_grad[...] = jnp.dot(grad_logits, w2_self, preferred_element_type=jnp.float32)
         grad_w1[...] = jnp.zeros_like(grad_w1)
 
-        @pl.loop(0, middle // seeds)
+        @pl.loop(0, middle // seeds, unroll=3)
         def _(part):
             rows = pl.ds(pl.multiple_of(part * seeds, seeds), seeds)
             seen = counts_t[pl.ds(part * (seeds // unit), seeds // unit)].reshape(seeds, seeds)
@@ -217,7 +220,6 @@
     steps = middle // block
     unit, units = 16, 4
     table_rows = hot_rows.shape[0] + cold_rows.shape[0] * cold_rows.shape[1]
-    positions = nbr1.reshape(fan_first, steps, block).transpose(1, 0, 2).reshape(-1)
     vmem = pl.BlockSpec(memory_space=pltpu.VMEM)
     smem = pl.BlockSpec(memory_space=pltpu.SMEM)
     rows_buffer = pltpu.VMEM((units, unit, width), jnp.float32)
@@ -231,7 +233,7 @@
         in_specs=[
             smem,
             smem,
-            pl.BlockSpec((fan_first * block,), lambda i: (i,), memory_space=pltpu.SMEM),
+            pl.BlockSpec((fan_first, 1, block), lambda i: (0, 0, i), memory_space=pltpu.SMEM),
         ]
         + [vmem] * 8,
         out_specs=(vmem, vmem),
@@ -252,11 +254,11 @@
             pltpu.VMEM((2, 256, hidden), jnp.bfloat16),
             pltpu.VMEM((2 * width, hidden), jnp.float32),
         ],
-        compiler_params=pltpu.CompilerParams(vmem_limit_bytes=52 * 1024 * 1024),
+        compiler_params=pltpu.CompilerParams(vmem_limit_bytes=40 * 1024 * 1024),
         name="sage_step",
     )(
-        counts, mid_self.reshape(-1), positions,
-        hot_rows, cold_rows, nbr2, labels, w1_self, w1_neigh, w2_self.T, w2_neigh.T,
+        counts, mid_self, nbr1.transpose(1, 0, 2),
+        hot_rows, cold_rows, nbr2.transpose(1, 0, 2), labels, w1_self, w1_neigh, w2_self.T, w2_neigh.T,
     )
 
 
@@ -265,10 +267,12 @@
     groups,
     hot_table,
     cold_table,
+    hot_ids,
+    cold_ids,
+    hot_out,
+    cold_out,
     hot_ids_ref,
     cold_ids_ref,
-    hot_out,
-    cold_out,
     hot_raw,
     cold_raw,
     hot_wide,
@@ -298,6 +302,12 @@
     def group_at(d):
         return (c, lax.rem(g + d, groups))
 
+    load_ids = [
+        pltpu.make_async_copy(hot_ids, hot_ids_ref, local_sems.at[4]),
+        pltpu.make_async_copy(cold_ids, cold_ids_ref, local_sems.at[5]),
+    ]
+    for load in load_ids:
+        load.start()
     load_cold = pltpu.make_async_copy(cold_table, cold_raw, local_sems.at[0])
     load_hot = pltpu.make_async_copy(hot_table, hot_raw, local_sems.at[1])
     load_cold.start()
@@ -313,6 +323,8 @@
     def _(d):
         pl.semaphore_signal(barrier, inc=1, device_id=group_at(d), device_id_type=MESH)
 
+    for load in load_ids:
+        load.wait()
     for j in range(cliques):
         hot_ask[j] = hot_ids_ref[0, j : j + 1, :]
     for o in range(groups):
@@ -369,11 +381,15 @@
 
     def gather(wide, wanted, who, stage):
         units, unit, width = stage.shape
-
-        @pl.loop(0, units)
+        slots = units * unit
+        span = min(slots, 128)
+
+        @pl.loop(0, slots // span)
         def _(part):
-            for r in range(unit):
-                stage[part, r : r + 1, :] = wide[pl.ds(wanted[who, 0, part * unit + r], 1), :]
+            near = wanted.at[who, 0, pl.ds(pl.multiple_of(part * span, span), span)]
+            for r in range(span):
+                at = part * (span // unit) + r // unit
+                stage[at, r % unit : r % unit + 1, :] = wide[pl.ds(near[r], 1), :]
 
         return stage[...].reshape(units * unit, width).astype(jnp.bfloat16)
 
@@ -388,8 +404,9 @@
     to_scalars.start()
     to_scalars.wait()
 
-    @pl.loop(1, groups)
-    def _(d):
+    @pl.loop(0, groups - 1)
+    def _(e):
+        d = lax.rem(e + groups // 2 - 1, groups - 1) + 1
         peer = lax.rem(g + groups - d, groups)
         cold_send[peer] = gather(cold_wide, cold_req_s, peer, cold_stage)
         give_cold(d).start()
@@ -427,7 +444,7 @@
     width = hot_shard.shape[1]
     hot_slots, cold_slots = hot_ids.shape[2], cold_ids.shape[2]
     vmem = pl.BlockSpec(memory_space=pltpu.VMEM)
-    anywhere = pl.BlockSpec(memory_space=pl.ANY)
+    hbm = pl.BlockSpec(memory_space=pltpu.HBM)
     bf16, f32, i32 = jnp.bfloat16, jnp.float32, jnp.int32
     return pl.pallas_call(
         partial(fetch_kernel, cliques, groups),
@@ -435,9 +452,11 @@
             jax.ShapeDtypeStruct((cliques, hot_slots, width), bf16),
             jax.ShapeDtypeStruct((groups, cold_slots, width), bf16),
         ),
-        in_specs=[anywhere, anywhere, vmem, vmem],
+        in_specs=[hbm, hbm, hbm, hbm],
         out_specs=(vmem, vmem),
         scratch_shapes=[
+            pltpu.VMEM(hot_ids.shape, i32),
+            pltpu.VMEM(cold_ids.shape, i32),
             pltpu.VMEM(hot_shard.shape, bf16),
             pltpu.VMEM(cold_shard.shape, bf16),
             pltpu.VMEM(hot_shard.shape, f32),
@@ -452,14 +471,14 @@
             pltpu.VMEM((cold_slots // 16, 16, width), f32),
             pltpu.VMEM((cliques, hot_slots, width), bf16),
             pltpu.VMEM((groups, cold_slots, width), bf16),
-            pltpu.SemaphoreType.DMA((4,)),
+            pltpu.SemaphoreType.DMA((6,)),
             pltpu.SemaphoreType.DMA((2, cliques - 1)),
             pltpu.SemaphoreType.DMA((2, groups - 1)),
             pltpu.SemaphoreType.DMA((2, cliques - 1)),
             pltpu.SemaphoreType.DMA((2, groups - 1)),
         ],
         compiler_params=pltpu.CompilerParams(
-            collective_id=1, has_side_effects=True, vmem_limit_bytes=48 * 1024 * 1024
+            collective_id=1, has_side_effects=True, vmem_limit_bytes=102 * 512 * 1024
         ),
         name="fetch_rows",
     )(hot_shard, cold_shard, hot_ids, cold_ids)
@@ -524,9 +543,11 @@
     for device in partners:
         pl.semaphore_signal(barrier, inc=1, device_id=device, device_id_type=MESH)
     terms = term_ref.shape[0]
-    whole[0:terms, :] = term_ref[...]
+    given = term_ref
     if rows > terms:
+        whole[0:terms, :] = term_ref[...]
         whole[terms:rows, :] = jnp.zeros((rows - terms, 128), jnp.float32)
+        given = whole
     pl.semaphore_wait(barrier, len(partners))
 
     pair_start = core * per_pair
@@ -534,11 +555,11 @@
     own = mine + chip * per_chip
 
     copy = send(
-        whole.at[rows_at((1 - core) * per_pair, per_pair)], pair_in, pair_sems, 0, pair()
+        given.at[rows_at((1 - core) * per_pair, per_pair)], pair_in, pair_sems, 0, pair()
     )
     copy.wait()
     half = rows_at(pair_start, per_pair)
-    half_sum[half, :] = whole[half, :] + pair_in[...]
+    half_sum[half, :] = given[half, :] + pair_in[...]
 
     copies = []
     for d in range(1, cliques):

time: 152 us -> 130 us (0.86)
  Pallas kernels: 140 us -> 125 us
  local copies, waits for them, and re-layouts: 8.49 us -> 4.08 us
  other arithmetic: 2.54 us -> 0 us
    pallas_call x1, Pallas kernels: 90.5 us -> 79.2 us  [sage_step(): pl.pallas_call(sage_kernel, grid=(steps,), out_shape=(jax.ShapeDtypeStruc...]
    pallas_call x1, Pallas kernels: 26.1 us -> 21.4 us  [fetch_rows(): pl.pallas_call(partial(fetch_kernel, cliques, groups), out_shape=(jax.Sha...]
    unnamed x25 -> x26, local copies, waits for them, and re-layouts: 8.1 us -> 4.08 us
    unnamed x2 -> x0, other arithmetic: 2.54 us -> none
where the time goes in v4:
time: 130 us
  Pallas kernels  125 us (96%)
  local copies, waits for them, and re-layouts  4.08 us (3%)
    pallas_call x1, Pallas kernels, sage_step(): pl.pallas_call(sage_kernel, grid=(steps,), out_shape=(jax.ShapeDtypeStruc...  79.2 us
    pallas_call x1, Pallas kernels, reduce_terms(): pl.pallas_call(partial(reduce_kernel, cliques, groups), out_shape=tuple((...  24.2 us
    pallas_call x1, Pallas kernels, fetch_rows(): pl.pallas_call(partial(fetch_kernel, cliques, groups), out_shape=(jax.Sha...  21.4 us
    unnamed x26, local copies, waits for them, and re-layouts  4.08 us

profile of v4, /device:TPU:0, one launch (start us, length us, event | category | flops | bytes accessed | tf_op | source)
XLA Modules:
  0.0 129.7 jit_solution(8138402244888406524)
XLA Ops:
  0.6 0.0 copy-start.7
  0.6 0.7 copy-done.7
  1.3 0.0 copy-start.8
  1.3 0.7 copy-done.8
  2.0 0.0 copy-start
  2.0 0.0 copy-start.1
  2.0 0.0 copy-start.2
  2.0 0.0 copy-start.3
  2.0 0.0 copy-start.4
  2.1 0.0 copy-start.5
  2.1 0.0 copy-start.6
  2.1 0.0 copy-start.9
  2.1 0.0 copy-start.10
  2.1 21.4 %fetch_rows.1 = (bf16[4,512,128]{2,1,0:T(8,128)(2,1)S(1)}, bf16[8,256,128]{2,1,0:T(8,128)(2,1)S(1)}) custom-call(bf16[16384,128]{1,0:T(8,128)(2,1)} %hot_table.1, bf16[16384,128]{1,0:T(8,128)(2,1)} %cold_table.1, s32[1,4,512]{2,1,0:T(4,128)S(1)} %copy-done.7, s32[1,8,256]{2,1,0:T(8,128)S(1)} %copy-done.8), custom_call_target="tpu_custom_call" | custom-call | tf_op jit(solution)/shard_map/fetch_rows/pallas_call | solution.py:449
  23.5 0.0 copy-done
  23.6 0.0 copy-done.1
  23.6 0.0 copy-done.2
  23.6 0.0 copy-done.3
  23.6 0.0 copy-done.4
  23.6 0.0 copy-done.5
  23.6 0.0 copy-done.6
  23.6 0.0 copy-done.9
  23.6 0.0 copy-done.10
  23.6 79.2 %sage_step.1 = (f32[1,512]{1,0:T(1,128)}, f32[1280,128]{1,0:T(8,128)S(1)}) custom-call(s32[1,8]{1,0:T(1,128)S(1)} %copy-done.10, s32[1,7680]{1,0:T(1,128)S(1)} %copy-done.5, s32[10,1,7680]{2,1,0:T(1,128)S(1)} %bitcast.8, bf16[2048,128]{1,0:T(8,128)(2,1)S(1)} %bitcast.7, bf16[8,256,128]{2,1,0:T(8,128)(2,1)S(1)} %get-tuple-element.14.cold_ref, ...), custom_call_target="tpu_custom_call" | custom-call | tf_op jit(solution)/shard_map/sage_step/pallas_call | solution.py:226
  102.8 24.2 %reduce_terms.1 = (f32[128,256]{1,0:T(8,128)S(1)}, f32[128,256]{1,0:T(8,128)S(1)}, f32[172,256]{1,0:T(8,128)S(1)}, f32[172,256]{1,0:T(8,128)S(1)}) custom-call(f32[1280,128]{1,0:T(8,128)S(1)} %get-tuple-element.16.term_ref), custom_call_target="tpu_custom_call" | custom-call | tf_op jit(solution)/shard_map/reduce_terms/pallas_call | solution.py:629
  127.0 0.7 copy.22
  127.7 0.7 copy.23
  128.3 0.7 copy.24
  129.0 0.7 copy.25
Async XLA Ops:
  0.6 0.7 copy-start.7
  1.3 0.7 copy-start.8
  2.0 21.5 %copy-start = (s32[1,10,7680]{2,0,1:T(1,128)S(1)}, s32[1,10,7680]{2,0,1:T(1,128)}, u32[]{:S(2)}) copy-start(s32[1,10,7680]{2,0,1:T(1,128)} %param.19) | copy-start | bytes 921604
  2.0 21.5 %copy-start.1 = (bf16[256,172]{0,1:T(8,128)(2,1)S(1)}, bf16[256,172]{0,1:T(8,128)(2,1)}, u32[]{:S(2)}) copy-start(bf16[256,172]{0,1:T(8,128)(2,1)} %param.24) | copy-start | bytes 264196
  2.0 21.5 %copy-start.2 = (bf16[256,172]{0,1:T(8,128)(2,1)S(1)}, bf16[256,172]{0,1:T(8,128)(2,1)}, u32[]{:S(2)}) copy-start(bf16[256,172]{0,1:T(8,128)(2,1)} %param.25) | copy-start | bytes 264196
  2.0 21.5 %copy-start.3 = (bf16[128,256]{1,0:T(8,128)(2,1)S(1)}, bf16[128,256]{1,0:T(8,128)(2,1)}, u32[]{:S(2)}) copy-start(bf16[128,256]{1,0:T(8,128)(2,1)} %w1_self_ref.1) | copy-start | bytes 196612
  2.0 21.5 %copy-start.4 = (bf16[128,256]{1,0:T(8,128)(2,1)S(1)}, bf16[128,256]{1,0:T(8,128)(2,1)}, u32[]{:S(2)}) copy-start(bf16[128,256]{1,0:T(8,128)(2,1)} %w1_neigh_ref.1) | copy-start | bytes 196612
  2.1 21.5 %copy-start.5 = (s32[1,7680]{1,0:T(1,128)S(1)}, s32[1,7680]{1,0:T(1,128)}, u32[]{:S(2)}) copy-start(s32[1,7680]{1,0:T(1,128)} %self_ref.1) | copy-start | bytes 92164
  2.1 21.5 %copy-start.6 = (s32[1,15,512]{2,0,1:T(1,128)S(1)}, s32[1,15,512]{2,0,1:T(1,128)}, u32[]{:S(2)}) copy-start(s32[1,15,512]{2,0,1:T(1,128)} %param.20) | copy-start | bytes 92164
  2.1 21.5 %copy-start.9 = (s32[1,512]{1,0:T(1,128)S(1)}, s32[1,512]{1,0:T(1,128)}, u32[]{:S(2)}) copy-start(s32[1,512]{1,0:T(1,128)} %labels_ref.1) | copy-start | bytes 6148
  2.1 21.5 %copy-start.10 = (s32[1,8]{1,0:T(1,128)S(1)}, s32[1,8]{1,0:T(1,128)}, u32[]{:S(2)}) copy-start(s32[1,8]{1,0:T(1,128)} %counts_ref.1) | copy-start | bytes 100
